TPU v7x, 512 devices: a whole 4x8x8 slice. The times are simulated.
512 devices in a mesh: depth: 16 (over z_lo, x, core), row: 8 (over y), col: 4 (over z_hi).
Axes of the slice: x: 4, y: 8, z: 8 (z_hi: 4, z_lo: 2; z = z_hi * 2 + z_lo), core: 2. Of those that a mesh axis runs over, the one named last changes fastest.
Arguments:
- inputs: bfloat16 [2048, 24576], P(('depth', 'row'), 'col'), may hold values from -0.5 to 0.5
- grad_out: bfloat16 [2048, 6144], P(('depth', 'col'), 'row'), may hold values from -16 to 16
- weight: bfloat16 [4, 6144, 6144], P('col', 'depth', 'row'), may hold values from -0.078125 to 0.078125
Outputs:
- grad_inputs: bfloat16 [2048, 24576], P(('depth', 'row'), 'col')
- grad_weight: bfloat16 [4, 6144, 6144], P('col', 'depth', 'row')
All inputs are finite; a program needn't handle non-finite values.
Results may differ from a plain program's by a relative error of at most 0.017.
Values may be sent and summed in bfloat16 or wider, within the bound.
No kernel may reach another device: no remote copies, remote signals or barrier semaphores. Data moves between devices by JAX's collectives and lax.ppermute only.
A program may use at most 64 MiB of HBM per device.

v0:
```python
import jax
import jax.numpy as jnp
from jax import lax
from jax.sharding import PartitionSpec as P


def round_term(values):
    return lax.optimization_barrier(values.astype(jnp.bfloat16)).astype(jnp.float32)


def local(inputs, grad_out, weight):
    slab_rows = lax.all_gather(grad_out, "col", axis=0, tiled=True)
    every_grad = lax.all_gather(slab_rows, "depth", axis=0, tiled=True)
    slab_acts = lax.all_gather(inputs, "row", axis=0, tiled=True)
    acts = lax.all_to_all(slab_acts, "depth", split_axis=1, concat_axis=0, tiled=True)
    weight_term = lax.dot_general(
        acts, every_grad, (((0,), (0,)), ((), ())), preferred_element_type=jnp.float32
    )
    grad_weight = weight_term.astype(jnp.bfloat16).reshape(weight.shape)
    tile_full = lax.all_gather(weight, "depth", axis=1, tiled=True)[0]
    grad_inputs = lax.psum_scatter(
        round_term(
            lax.dot_general(
                slab_rows, tile_full, (((1,), (1,)), ((), ())), preferred_element_type=jnp.float32
            )
        ).astype(jnp.bfloat16),
        "row",
        scatter_dimension=0,
        tiled=True,
    )
    return (grad_inputs, grad_weight)


def solution(mesh):
    in_specs = (P(("depth", "row"), "col"), P(("depth", "col"), "row"), P("col", "depth", "row"))
    out_specs = (P(("depth", "row"), "col"), P("col", "depth", "row"))
    return jax.shard_map(local, mesh=mesh, in_specs=in_specs, out_specs=out_specs, check_vma=False)
```

profile of v0, /device:TPU:1, one launch (start us, length us, event | category | flops | bytes accessed | tf_op | source)
XLA Modules:
  0.0 222.6 jit_solution(11339082768518053422)
XLA Ops:
  7.2 0.0 all-gather.6.cloned.1.call-start
  7.2 0.7 all-gather.6.cloned.1.call-update
  7.9 0.0 all-gather.4.cloned.1.call-start
  7.9 0.7 all-gather.4.cloned.1.call-update
  8.6 0.0 all-gather.8.cloned.1.call-start
  8.7 19.5 %all_gather.12 = bf16[128,768]{1,0:T(8,128)(2,1)} all-gather(bf16[32,768]{1,0:T(8,128)(2,1)} %param.4), channel_id=1, replica_groups=mesh['depth'=16,'row'=8,'col'=4] {'col'}, dimensions={0}, use_global_device_ids=true | all-gather | bytes 245760 | tf_op jit(solution)/shard_map/all_gather | solution.py:12
  28.1 0.0 all-gather.8.cloned.1.call-update
  28.2 25.9 %all-gather.6.cloned.1.call-done = bf16[128,6144]{1,0:T(8,128)(2,1)} async-done(((bf16[16,6144]{1,0:T(8,128)(2,1)}), bf16[128,6144]{1,0:T(8,128)(2,1)}) %all-gather.6.cloned.1.call-update) | async-done | bytes 1572880 | tf_op jit(solution)/shard_map/all_gather | solution.py:14
  54.0 2.6 %copy.7 = bf16[128,6144]{0,1:T(8,128)(2,1)} copy(bf16[128,6144]{1,0:T(8,128)(2,1)} %all-gather.6.cloned.1.call-done) | data formatting | bytes 3145728 | tf_op jit(solution)/shard_map/all_gather | solution.py:14
  56.6 0.0 copy-start
  56.6 10.2 %all-to-all-start = ((bf16[128,16,384]{0,2,1:T(8,128)(2,1)}), bf16[128,16,384]{0,2,1:T(8,128)(2,1)S(1)}, u32[]{:S(2)}, u32[]{:S(2)}) async-start(bf16[128,16,384]{0,2,1:T(8,128)(2,1)} %bitcast.1), calls=%async_computation.1 | async-start | bytes 3145728 | tf_op jit(solution)/shard_map/all_to_all | solution.py:15
  66.8 0.0 reduce-scatter.2.cloned.1.call-start
  66.9 65.8 %all-gather.4.cloned.1.call-done = bf16[1,6144,768]{2,1,0:T(8,128)(2,1)} async-done(((bf16[1,384,768]{2,1,0:T(8,128)(2,1)}), bf16[1,6144,768]{2,1,0:T(8,128)(2,1)}) %all-gather.4.cloned.1.call-update) | async-done | bytes 9437200 | tf_op jit(solution)/shard_map/all_gather | solution.py:20
  132.7 0.0 copy-done
  132.7 8.0 %fusion.2 = bf16[128,6144]{1,0:T(8,128)(2,1)} fusion(bf16[128,768]{1,0:T(8,128)(2,1)S(1)} %copy-done, bf16[1,6144,768]{2,1,0:T(8,128)(2,1)} %all-gather.4.cloned.1.call-done), kind=kOutput, calls=%fused_computation.2 | convolution fusion | flops 1208745984 | bytes 11206656 | tf_op jit(solution)/shard_map/dot_general | solution.py:23
  140.7 0.0 reduce-scatter.2.cloned.1.call-update
  140.7 0.0 all-to-all-done
  140.7 0.9 copy.8
  141.6 32.6 %all-gather.8.cloned.1.call-done = bf16[2048,768]{1,0:T(8,128)(2,1)} async-done(((bf16[128,768]{1,0:T(8,128)(2,1)}), bf16[2048,768]{1,0:T(8,128)(2,1)}) %all-gather.8.cloned.1.call-update) | async-done | bytes 3145744 | tf_op jit(solution)/shard_map/all_gather | solution.py:13
  174.3 4.1 %fusion.5 = bf16[1,384,768]{2,1,0:T(8,128)(2,1)} fusion(bf16[2048,384]{1,0:T(8,128)(2,1)S(1)} %bitcast.14, bf16[2048,768]{1,0:T(8,128)(2,1)} %all-gather.8.cloned.1.call-done), kind=kOutput, calls=%fused_computation.4 | convolution fusion | flops 1208254464 | bytes 5308416 | tf_op jit(solution)/shard_map/dot_general | solution.py:16
  178.4 37.7 %reduce-scatter.2.cloned.1.call-done = bf16[16,6144]{1,0:T(8,128)(2,1)} async-done(((bf16[128,6144]{1,0:T(8,128)(2,1)}), bf16[16,6144]{1,0:T(8,128)(2,1)}) %reduce-scatter.2.cloned.1.call-update) | async-done | bytes 196624 | tf_op jit(solution)/shard_map/reduce_scatter | solution.py:21
Async XLA Ops:
  7.2 46.9 %all-gather.6.cloned.1.call-start = ((), (), s32[]{:S(2)}) async-start(), calls=%async_computation.4 | async-start | bytes 1769472 | tf_op jit(solution)/shard_map/all_gather | solution.py:14
  7.9 124.8 %all-gather.4.cloned.1.call-start = ((), (), s32[]{:S(2)}) async-start(), calls=%async_computation.2 | async-start | bytes 10027008 | tf_op jit(solution)/shard_map/all_gather | solution.py:20
  8.6 165.6 %all-gather.8.cloned.1.call-start = ((), (), s32[]{:S(2)}) async-start(), calls=%async_computation.5 | async-start | bytes 3342336 | tf_op jit(solution)/shard_map/all_gather | solution.py:13
  56.6 76.1 %copy-start = (bf16[128,768]{1,0:T(8,128)(2,1)S(1)}, bf16[128,768]{1,0:T(8,128)(2,1)}, u32[]{:S(2)}) copy-start(bf16[128,768]{1,0:T(8,128)(2,1)} %all_gather.12) | copy-start | bytes 589828
  56.6 84.1 %all-to-all-start = ((bf16[128,16,384]{0,2,1:T(8,128)(2,1)}), bf16[128,16,384]{0,2,1:T(8,128)(2,1)S(1)}, u32[]{:S(2)}, u32[]{:S(2)}) async-start(bf16[128,16,384]{0,2,1:T(8,128)(2,1)} %bitcast.1), calls=%async_computation.1 | async-start | bytes 3145728 | tf_op jit(solution)/shard_map/all_to_all | solution.py:15
  66.8 149.2 %reduce-scatter.2.cloned.1.call-start = ((), (), s32[]{:S(2)}) async-start(), calls=%async_computation.3 | async-start | bytes 1769472 | tf_op jit(solution)/shard_map/reduce_scatter | solution.py:21
Sparse Core Ops, SparseCore 0:
  10.1 43.9 all-gather.5
  56.2 76.5 all-gather.3
  134.9 39.3 all-gather.7
  177.5 38.4 reduce-scatter.1
where the time goes:
time: 226 us; the launch traced here: 223 us
  waiting for transfers between devices  163 us (72%)
  blocking collectives  19.5 us (9%)
  between operations  13.8 us (6%)
  matrix products  12.1 us (5%)
  starting transfers between devices  10.4 us (5%)
  local copies, waits for them, and re-layouts  3.47 us (2%)
    all_gather x1, waiting for transfers between devices, local(): tile_full = lax.all_gather(weight, 'depth', axis=1, tiled=True)[0]  65.8 us
    reduce_scatter x1, waiting for transfers between devices, local(): lax.psum_scatter(round_term(lax.dot_general(slab_rows, tile_full, (((1,),...  37.7 us
    all_gather x1, waiting for transfers between devices, local(): every_grad = lax.all_gather(slab_rows, 'depth', axis=0, tiled=True)  32.6 us
    all_gather x1, waiting for transfers between devices, local(): slab_acts = lax.all_gather(inputs, 'row', axis=0, tiled=True)  25.9 us
    all_gather x1, blocking collectives, local(): slab_rows = lax.all_gather(grad_out, 'col', axis=0, tiled=True)  19.5 us
    all_to_all x1, starting transfers between devices, local(): lax.all_to_all(slab_acts, 'depth', split_axis=1, concat_axis=0, tiled=True)  10.2 us
    dot_general x1, matrix products, local(): lax.dot_general(slab_rows, tile_full, (((1,), (1,)), ((), ())), preferred...  7.98 us
  transfers between devices with their start and end apart: 5, of which 4 were waited for; matrix products, arithmetic and copies ran while one was open for 7% of the time, Pallas kernels for 0%

commit v1 on v0

v1 whole, which is shorter than its diff:
```python
import jax
import jax.numpy as jnp
from jax import lax
from jax.experimental import pallas as pl
from jax.experimental.pallas import tpu as pltpu
from jax.sharding import PartitionSpec as P

NX, NZ, NC, NY = 4, 2, 4, 8
T, F, H = 16, 768, 768


def depth_of(zl, x, core):
    return (zl * NX + x) * 2 + core


def near_groups():
    return [
        [
            (depth_of(zl, x, core) * NY + 2 * y4 + yp) * NC + c
            for c in range(NC)
            for zl in range(NZ)
            for yp in range(2)
        ]
        for x in range(NX)
        for core in range(2)
        for y4 in range(NY // 2)
    ]


def x_groups():
    return [[depth_of(zl, x, core) for x in range(NX)] for zl in range(NZ) for core in range(2)]


def token_groups():
    return [
        [
            depth_of(zl, x, core) * NY + 2 * y4 + parity
            for x in range(NX)
            for y4 in range(NY // 2)
            for zl in range(NZ)
        ]
        for core in range(2)
        for parity in range(2)
    ]


def call(kernel, out_shape, scalars, *operands):
    n = len(operands)
    return pl.pallas_call(
        kernel,
        out_shape=out_shape,
        in_specs=[pl.BlockSpec(memory_space=pltpu.SMEM)]
        + [pl.BlockSpec(memory_space=pltpu.VMEM)] * n,
        out_specs=jax.tree.map(lambda _: pl.BlockSpec(memory_space=pltpu.VMEM), out_shape),
        compiler_params=pltpu.CompilerParams(vmem_limit_bytes=48 * 1024 * 1024),
    )(scalars, *operands)


def spread_kernel(s_ref, x_ref, o_ref):
    for zl in range(NZ):
        for x in range(NX):
            block = x_ref[:, pl.ds((zl * NX + x) * H, H)]
            for y4 in range(NY // 2):
                o_ref[x, y4, zl] = block


def terms_kernel(s_ref, g_ref, own_ref, other_ref, o_ref):
    parity = s_ref[0]
    g_own = g_ref[:, parity].reshape(32 * T, F)
    g_other = g_ref[:, 1 - parity].reshape(32 * T, F)
    for half in range(2):
        total = lax.dot_general(
            g_own, own_ref[half], (((1,), (1,)), ((), ())), preferred_element_type=jnp.float32
        ) + lax.dot_general(
            g_other, other_ref[half], (((1,), (1,)), ((), ())), preferred_element_type=jnp.float32
        )
        o_ref[:, :, pl.ds(half * 384, 384)] = total.astype(jnp.bfloat16).reshape(32, T, 384)


def weight_kernel(flip, s_ref, a_ref, g_ref, o_ref):
    parity, core = s_ref[0], s_ref[1]
    h0 = pl.multiple_of((1 - core if flip else core) * 384, 384)
    acts = a_ref[:, pl.ds(h0, 384)]
    for k in range(2):
        g = g_ref[:, 1 - parity if k else parity].reshape(32 * T, F)
        o_ref[k] = lax.dot_general(
            acts, g, (((0,), (0,)), ((), ())), preferred_element_type=jnp.float32
        ).astype(o_ref.dtype)


def sum_kernel(s_ref, x_ref, o_ref):
    for zl in range(NZ):
        for x in range(NX):
            total = x_ref[x, 0, zl].astype(jnp.float32)
            for y4 in range(1, NY // 2):
                total = total + x_ref[x, y4, zl].astype(jnp.float32)
            o_ref[:, pl.ds((zl * NX + x) * H, H)] = total.astype(jnp.bfloat16)


def swap_core(x):
    return lax.ppermute(x, "depth", [(i, i ^ 1) for i in range(16)])


def swap_pair(x):
    return lax.ppermute(x, "row", [(i, i ^ 1) for i in range(8)])


def local(inputs, grad_out, weight):
    bf = jnp.bfloat16
    core = lax.axis_index("depth") % 2
    parity = lax.axis_index("row") % 2
    s = jnp.stack([parity, core]).astype(jnp.int32)

    w = weight.reshape(384, F)
    w_pair = swap_pair(w)
    near = lax.all_to_all(
        jnp.broadcast_to(grad_out.reshape(1, 2, T, F), (8, 2, T, F)).reshape(16, T, F),
        ("depth", "row", "col"),
        split_axis=0,
        concat_axis=0,
        axis_index_groups=near_groups(),
        tiled=True,
    )
    spread = call(
        spread_kernel, jax.ShapeDtypeStruct((NX, NY // 2, NZ, T, H), bf), s, inputs
    ).reshape(32, T, H)
    acts = lax.all_to_all(
        spread,
        ("depth", "row"),
        split_axis=0,
        concat_axis=0,
        axis_index_groups=token_groups(),
        tiled=True,
    ).reshape(32 * T, H)
    grads = lax.all_to_all(
        jnp.broadcast_to(near.reshape(1, 16 * T, F), (NX, 16 * T, F)),
        "depth",
        split_axis=0,
        concat_axis=0,
        axis_index_groups=x_groups(),
        tiled=True,
    ).reshape(32, 2, T, F)
    w_core, w_both = swap_core(w), swap_core(w_pair)

    def by_core(mine, theirs):
        return jnp.where(core == 0, jnp.stack([mine, theirs]), jnp.stack([theirs, mine]))

    own, other = by_core(w, w_core), by_core(w_pair, w_both)
    terms = call(terms_kernel, jax.ShapeDtypeStruct((32, T, H), bf), s, grads, own, other)
    summed = lax.all_to_all(
        terms,
        ("depth", "row"),
        split_axis=0,
        concat_axis=0,
        axis_index_groups=token_groups(),
        tiled=True,
    )

    def weight_term(flip, dtype):
        return call(
            lambda *refs: weight_kernel(flip, *refs),
            jax.ShapeDtypeStruct((2, 384, F), dtype),
            s,
            acts,
            grads,
        )

    sent = swap_core(weight_term(True, bf))
    kept = weight_term(False, jnp.float32)
    both = kept + sent.astype(jnp.float32)
    crossed = swap_pair(both[1].astype(bf))
    grad_weight = (both[0] + crossed.astype(jnp.float32)).astype(bf)
    grad_inputs = call(
        sum_kernel,
        jax.ShapeDtypeStruct((T, 8 * H), bf),
        s,
        summed.reshape(NX, NY // 2, NZ, T, H),
    )
    return grad_inputs, grad_weight.reshape(weight.shape)


def solution(mesh):
    in_specs = (P(("depth", "row"), "col"), P(("depth", "col"), "row"), P("col", "depth", "row"))
    out_specs = (P(("depth", "row"), "col"), P("col", "depth", "row"))
    return jax.shard_map(local, mesh=mesh, in_specs=in_specs, out_specs=out_specs, check_vma=False)
```

time: 226 us -> 136 us (0.60); the launches traced: 223 us -> 136 us
  waiting for transfers between devices: 163 us -> 35.9 us
  starting transfers between devices: 10.4 us -> 51.6 us
  between operations: 13.8 us -> 0.79 us
  matrix products: 12.1 us -> 0 us
  Pallas kernels: 0 us -> 8.89 us
  blocking collectives: 19.5 us -> 27.9 us
  other arithmetic: 0 us -> 6.85 us
    all_gather x3 -> x0, waiting for transfers between devices: 124 us -> none  [the longest x1 65.8 us: local(): tile_full = lax.all_gather(weight, 'depth', axis=1, tiled=True)[0]]
    reduce_scatter x1 -> x0, waiting for transfers between devices: 37.7 us -> none  [local(): lax.psum_scatter(round_term(lax.dot_general(slab_rows, tile_full, (((1,),...]
    ppermute x0 -> x5, starting transfers between devices: none -> 32 us  [the longest x2 17.1 us: swap_pair(): return lax.ppermute(x, 'row', [(i, i ^ 1) for i in range(8)])]
    all_to_all x0 -> x1, blocking collectives: none -> 27.9 us  [local(): lax.all_to_all(spread, ('depth', 'row'), split_axis=0, concat_axis=0, axi...]
    all_to_all x1 -> x3, waiting for transfers between devices: 0.01 us -> 24.9 us  [the longest x1 11.8 us: local(): lax.all_to_all(jnp.broadcast_to(grad_out.reshape(1, 2, T, F), (8, 2, T, F...]
    all_gather x1 -> x0, blocking collectives: 19.5 us -> none  [local(): slab_rows = lax.all_gather(grad_out, 'col', axis=0, tiled=True)]
    dot_general x2 -> x0, matrix products: 12.1 us -> none  [the longest x1 7.98 us: local(): lax.dot_general(slab_rows, tile_full, (((1,), (1,)), ((), ())), preferred...]
    ppermute x0 -> x5, waiting for transfers between devices: none -> 11 us  [the longest x2 10.5 us: swap_pair(): return lax.ppermute(x, 'row', [(i, i ^ 1) for i in range(8)])]
  transfers between devices with their start and end apart: 5 -> 8, of which waited for: 4 -> 5; matrix products, arithmetic and copies ran while one was open for 7% -> 4% of each run, Pallas kernels for 0% -> 7%
where the time goes in v1:
time: 136 us
  starting transfers between devices  51.6 us (38%)
  waiting for transfers between devices  35.9 us (26%)
  blocking collectives  27.9 us (21%)
  Pallas kernels  8.89 us (7%)
  other arithmetic  6.85 us (5%)
  local copies, waits for them, and re-layouts  3.77 us (3%)
    all_to_all x1, blocking collectives, local(): lax.all_to_all(spread, ('depth', 'row'), split_axis=0, concat_axis=0, axi...  27.9 us
    ppermute x2, starting transfers between devices, swap_pair(): return lax.ppermute(x, 'row', [(i, i ^ 1) for i in range(8)])  17.1 us
    ppermute x3, starting transfers between devices, swap_core(): return lax.ppermute(x, 'depth', [(i, i ^ 1) for i in range(16)])  14.9 us
    all_to_all x1, starting transfers between devices, local(): lax.all_to_all(jnp.broadcast_to(grad_out.reshape(1, 2, T, F), (8, 2, T, F...  12 us
    all_to_all x1, waiting for transfers between devices, local(): lax.all_to_all(jnp.broadcast_to(grad_out.reshape(1, 2, T, F), (8, 2, T, F...  11.8 us
    ppermute x2, waiting for transfers between devices, swap_pair(): return lax.ppermute(x, 'row', [(i, i ^ 1) for i in range(8)])  10.5 us
    pallas_call x5, Pallas kernels, call(): pl.pallas_call(kernel, out_shape=out_shape, in_specs=[pl.BlockSpec(memory...  8.89 us
    all_to_all x1, waiting for transfers between devices, local(): lax.all_to_all(terms, ('depth', 'row'), split_axis=0, concat_axis=0, axis...  8.31 us
  transfers between devices with their start and end apart: 8, of which 5 were waited for; matrix products, arithmetic and copies ran while one was open for 4% of the time, Pallas kernels for 7%

profile of v1, /device:TPU:1, one launch (start us, length us, event | category | flops | bytes accessed | tf_op | source)
XLA Modules:
  0.0 135.7 jit_solution(2085806065796688852)
XLA Ops:
  0.6 0.0 copy-start
  0.6 1.6 %broadcast_in_dim.15 = bf16[8,2,16,768]{3,2,1,0:T(8,128)(2,1)} broadcast(bf16[2,16,768]{2,1,0:T(8,128)(2,1)} %bitcast.35), dimensions={1,2,3} | broadcast | bytes 442368 | tf_op jit(solution)/shard_map/broadcast_in_dim | solution.py:117
  2.3 12.0 %all-to-all-start = ((bf16[16,16,768]{2,1,0:T(8,128)(2,1)}), bf16[16,16,768]{2,1,0:T(8,128)(2,1)S(1)}, u32[]{:S(2)}, u32[]{:S(2)}) async-start(bf16[16,16,768]{2,1,0:T(8,128)(2,1)} %bitcast.3), calls=%async_computation | async-start | bytes 786432 | tf_op jit(solution)/shard_map/all_to_all | solution.py:116
  14.3 0.1 pad_add_fusion.s_ref.refs_0_
  14.3 0.0 copy-done
  14.3 0.6 shard_map.52
  14.9 11.8 %all-to-all-done = bf16[16,16,768]{2,1,0:T(8,128)(2,1)S(1)} async-done(((bf16[16,16,768]{2,1,0:T(8,128)(2,1)}), bf16[16,16,768]{2,1,0:T(8,128)(2,1)S(1)}, u32[]{:S(2)}, u32[]{:S(2)}) %all-to-all-start) | async-done | bytes 393248 | tf_op jit(solution)/shard_map/all_to_all | solution.py:116
  26.7 27.9 %all_to_all.20 = bf16[32,16,768]{2,1,0:T(8,128)(2,1)S(1)} all-to-all(bf16[32,16,768]{2,1,0:T(8,128)(2,1)S(1)} %bitcast.31), channel_id=1, replica_groups={{0,256,8,264,16,272,24,280,64,320,72,328,80,336,88,344,128,384,136,392,..., dimensions={0} | all-to-all | bytes 1572864 | tf_op jit(solution)/shard_map/all_to_all | solution.py:127
  54.6 1.3 broadcast_in_dim.17
  55.9 0.0 copy-start.1
  55.9 3.7 %all-to-all-start.1 = ((bf16[4,256,768]{2,1,0:T(8,128)(2,1)}), bf16[4,256,768]{2,1,0:T(8,128)(2,1)S(1)}, u32[]{:S(2)}, u32[]{:S(2)}) async-start(bf16[4,256,768]{2,1,0:T(8,128)(2,1)} %broadcast_in_dim.17), calls=%async_computation.1 | async-start | bytes 3145728 | tf_op jit(solution)/shard_map/all_to_all | solution.py:135
  59.6 0.0 copy-done.1
  59.6 8.2 %collective-permute-start.1 = (bf16[384,768]{1,0:T(8,128)(2,1)S(1)}, bf16[384,768]{1,0:T(8,128)(2,1)}, u32[]{:S(2)}, u32[]{:S(2)}) collective-permute-start(bf16[384,768]{1,0:T(8,128)(2,1)S(1)} %bitcast.33), channel_id=1, source_target_pairs={{0,4},{4,0},{8,12},{12,8},{16,20},{20,16},{24,28},{28,24},{1,5},{5... | collective-permute-start | bytes 1769480 | tf_op jit(solution)/shard_map/ppermute | solution.py:105
  67.8 4.8 %all-to-all-done.1 = bf16[4,256,768]{2,1,0:T(8,128)(2,1)S(1)} async-done(((bf16[4,256,768]{2,1,0:T(8,128)(2,1)}), bf16[4,256,768]{2,1,0:T(8,128)(2,1)S(1)}, u32[]{:S(2)}, u32[]{:S(2)}) %all-to-all-start.1) | async-done | bytes 1572896 | tf_op jit(solution)/shard_map/all_to_all | solution.py:135
  72.6 2.4 %shard_map.54 = bf16[2,384,768]{2,1,0:T(8,128)(2,1)} custom-call(s32[2]{0:T(128)S(1)} %pad_add_fusion.s_ref.refs_0_, bf16[512,768]{1,0:T(8,128)(2,1)S(1)} %bitcast.28, bf16[32,2,16,768]{3,2,1,0:T(8,128)(2,1)S(1)} %bitcast.25), custom_call_target="tpu_custom_call" | custom-call | tf_op jit(solution)/shard_map/pallas_call | solution.py:49
  75.0 10.6 %collective-permute-start.3 = (bf16[2,384,768]{2,1,0:T(8,128)(2,1)}, bf16[2,384,768]{2,1,0:T(8,128)(2,1)}, u32[]{:S(2)}, u32[]{:S(2)}) collective-permute-start(bf16[2,384,768]{2,1,0:T(8,128)(2,1)} %shard_map.54), channel_id=1, source_target_pairs={{0,32},{32,0},{64,96},{96,64},{128,160},{160,128},{192,224},{224,1... | collective-permute-start | bytes 3538952 | tf_op jit(solution)/shard_map/ppermute | solution.py:101
  85.6 1.9 %collective-permute-start = (bf16[384,768]{1,0:T(8,128)(2,1)S(1)}, bf16[384,768]{1,0:T(8,128)(2,1)}, u32[]{:S(2)}, u32[]{:S(2)}) collective-permute-start(bf16[384,768]{1,0:T(8,128)(2,1)S(1)} %bitcast.34), channel_id=1, source_target_pairs={{0,32},{32,0},{64,96},{96,64},{128,160},{160,128},{192,224},{224,1... | collective-permute-start | bytes 1769480 | tf_op jit(solution)/shard_map/ppermute | solution.py:101
  87.5 0.0 collective-permute-done.1
  87.5 2.4 %collective-permute-start.2 = (bf16[384,768]{1,0:T(8,128)(2,1)}, bf16[384,768]{1,0:T(8,128)(2,1)}, u32[]{:S(2)}, u32[]{:S(2)}) collective-permute-start(bf16[384,768]{1,0:T(8,128)(2,1)} %collective-permute-done.1), channel_id=1, source_target_pairs={{0,32},{32,0},{64,96},{96,64},{128,160},{160,128},{192,224},{224,1... | collective-permute-start | bytes 1769480 | tf_op jit(solution)/shard_map/ppermute | solution.py:101
  89.9 0.0 collective-permute-done
  89.9 1.4 %maximum_select_fusion.own_ref = bf16[2,384,768]{2,1,0:T(8,128)(2,1)S(1)} fusion(bf16[1,384,768]{2,1,0:T(8,128)(2,1)} %bitcast.7, bf16[1,384,768]{2,1,0:T(8,128)(2,1)S(1)} %copy-done.1, pred[]{:T(512)S(6)} %eq.7), kind=kLoop, calls=%fused_computation.5 | loop fusion | flops 1769472 | bytes 2359297 | tf_op jit(solution)/shard_map/jit(_where)/select_n | solution.py:146
  91.4 0.5 collective-permute-done.2
  91.9 1.8 %maximum_select_fusion.1.other_ref = bf16[2,384,768]{2,1,0:T(8,128)(2,1)S(1)} fusion(bf16[1,384,768]{2,1,0:T(8,128)(2,1)} %bitcast.9, bf16[1,384,768]{2,1,0:T(8,128)(2,1)} %bitcast.8, pred[]{:T(512)S(6)} %eq.7), kind=kLoop, calls=%fused_computation.6 | loop fusion | flops 1769472 | bytes 2359297 | tf_op jit(solution)/shard_map/jit(_where)/select_n | solution.py:146
  93.7 3.2 %shard_map.50 = bf16[32,16,768]{2,1,0:T(8,128)(2,1)} custom-call(s32[2]{0:T(128)S(1)} %pad_add_fusion.s_ref.refs_0_, bf16[32,2,16,768]{3,2,1,0:T(8,128)(2,1)S(1)} %bitcast.26, bf16[2,384,768]{2,1,0:T(8,128)(2,1)S(1)} %maximum_select_fusion.own_ref, bf16[2,384,768]{2,1,0:T(8,128)(2,1)S(1)} %maximum_select_fusion.1.other_ref), custom_call_target="tpu_custom_call" | custom-call | tf_op jit(solution)/shard_map/pallas_call | solution.py:49
  96.9 3.9 %all-to-all-start.2 = ((bf16[32,16,768]{2,1,0:T(8,128)(2,1)}), bf16[32,16,768]{2,1,0:T(8,128)(2,1)S(1)}, u32[]{:S(2)}, u32[]{:S(2)}) async-start(bf16[32,16,768]{2,1,0:T(8,128)(2,1)} %shard_map.50), calls=%async_computation.2 | async-start | bytes 1572864 | tf_op jit(solution)/shard_map/all_to_all | solution.py:150
  100.8 1.4 %shard_map.53 = f32[2,384,768]{2,1,0:T(8,128)S(1)} custom-call(s32[2]{0:T(128)S(1)} %pad_add_fusion.s_ref.refs_0_, bf16[512,768]{1,0:T(8,128)(2,1)S(1)} %bitcast.29, bf16[32,2,16,768]{3,2,1,0:T(8,128)(2,1)S(1)} %bitcast.27), custom_call_target="tpu_custom_call" | custom-call | tf_op jit(solution)/shard_map/pallas_call | solution.py:49
  102.2 0.0 collective-permute-done.3
  102.2 1.5 %convert_add_fusion = f32[2,384,768]{2,1,0:T(8,128)S(1)} fusion(f32[2,384,768]{2,1,0:T(8,128)S(1)} %shard_map.53, bf16[2,384,768]{2,1,0:T(8,128)(2,1)} %collective-permute-done.3), kind=kLoop, calls=%fused_computation | loop fusion | flops 1179648 | bytes 5898240 | tf_op jit(solution)/shard_map/add | solution.py:170
  103.7 0.9 fusion.3
  104.6 8.9 %collective-permute-start.4 = (bf16[384,768]{1,0:T(8,128)(2,1)}, bf16[384,768]{1,0:T(8,128)(2,1)}, u32[]{:S(2)}, u32[]{:S(2)}) collective-permute-start(bf16[384,768]{1,0:T(8,128)(2,1)} %fusion.3), channel_id=1, source_target_pairs={{0,4},{4,0},{8,12},{12,8},{16,20},{20,16},{24,28},{28,24},{1,5},{5... | collective-permute-start | bytes 1769480 | tf_op jit(solution)/shard_map/ppermute | solution.py:105
  113.5 8.3 %all-to-all-done.2 = bf16[32,16,768]{2,1,0:T(8,128)(2,1)S(1)} async-done(((bf16[32,16,768]{2,1,0:T(8,128)(2,1)}), bf16[32,16,768]{2,1,0:T(8,128)(2,1)S(1)}, u32[]{:S(2)}, u32[]{:S(2)}) %all-to-all-start.2) | async-done | bytes 786464 | tf_op jit(solution)/shard_map/all_to_all | solution.py:150
  121.8 1.3 shard_map.51
  123.1 10.5 %collective-permute-done.4 = bf16[384,768]{1,0:T(8,128)(2,1)} collective-permute-done((bf16[384,768]{1,0:T(8,128)(2,1)}, bf16[384,768]{1,0:T(8,128)(2,1)}, u32[]{:S(2)}, u32[]{:S(2)}) %collective-permute-start.4) | collective-permute-done | bytes 589856 | tf_op jit(solution)/shard_map/ppermute | solution.py:105
  133.6 2.0 %fusion.2 = bf16[1,384,768]{2,1,0:T(8,128)(2,1)} fusion(bf16[384,768]{1,0:T(8,128)(2,1)} %collective-permute-done.4, f32[2,384,768]{2,1,0:T(8,128)S(1)} %convert_add_fusion), kind=kLoop, calls=%fused_computation.7 | loop fusion | flops 884736 | bytes 2359296 | tf_op jit(solution)/shard_map/reshape | solution.py:179
Async XLA Ops:
  0.6 13.7 %copy-start = (bf16[16,6144]{1,0:T(8,128)(2,1)S(1)}, bf16[16,6144]{1,0:T(8,128)(2,1)}, u32[]{:S(2)}) copy-start(bf16[16,6144]{1,0:T(8,128)(2,1)} %x_ref.1) | copy-start | bytes 589828
  2.3 24.5 %all-to-all-start = ((bf16[16,16,768]{2,1,0:T(8,128)(2,1)}), bf16[16,16,768]{2,1,0:T(8,128)(2,1)S(1)}, u32[]{:S(2)}, u32[]{:S(2)}) async-start(bf16[16,16,768]{2,1,0:T(8,128)(2,1)} %bitcast.3), calls=%async_computation | async-start | bytes 786432 | tf_op jit(solution)/shard_map/all_to_all | solution.py:116
  55.9 3.7 %copy-start.1 = (bf16[1,384,768]{2,1,0:T(8,128)(2,1)S(1)}, bf16[1,384,768]{2,1,0:T(8,128)(2,1)}, u32[]{:S(2)}) copy-start(bf16[1,384,768]{2,1,0:T(8,128)(2,1)} %param.5) | copy-start | bytes 1769476
  55.9 16.7 %all-to-all-start.1 = ((bf16[4,256,768]{2,1,0:T(8,128)(2,1)}), bf16[4,256,768]{2,1,0:T(8,128)(2,1)S(1)}, u32[]{:S(2)}, u32[]{:S(2)}) async-start(bf16[4,256,768]{2,1,0:T(8,128)(2,1)} %broadcast_in_dim.17), calls=%async_computation.1 | async-start | bytes 3145728 | tf_op jit(solution)/shard_map/all_to_all | solution.py:135
  59.6 27.9 %collective-permute-start.1 = (bf16[384,768]{1,0:T(8,128)(2,1)S(1)}, bf16[384,768]{1,0:T(8,128)(2,1)}, u32[]{:S(2)}, u32[]{:S(2)}) collective-permute-start(bf16[384,768]{1,0:T(8,128)(2,1)S(1)} %bitcast.33), channel_id=1, source_target_pairs={{0,4},{4,0},{8,12},{12,8},{16,20},{20,16},{24,28},{28,24},{1,5},{5... | collective-permute-start | bytes 1769480 | tf_op jit(solution)/shard_map/ppermute | solution.py:105
  75.0 27.2 %collective-permute-start.3 = (bf16[2,384,768]{2,1,0:T(8,128)(2,1)}, bf16[2,384,768]{2,1,0:T(8,128)(2,1)}, u32[]{:S(2)}, u32[]{:S(2)}) collective-permute-start(bf16[2,384,768]{2,1,0:T(8,128)(2,1)} %shard_map.54), channel_id=1, source_target_pairs={{0,32},{32,0},{64,96},{96,64},{128,160},{160,128},{192,224},{224,1... | collective-permute-start | bytes 3538952 | tf_op jit(solution)/shard_map/ppermute | solution.py:101
  85.6 4.4 %collective-permute-start = (bf16[384,768]{1,0:T(8,128)(2,1)S(1)}, bf16[384,768]{1,0:T(8,128)(2,1)}, u32[]{:S(2)}, u32[]{:S(2)}) collective-permute-start(bf16[384,768]{1,0:T(8,128)(2,1)S(1)} %bitcast.34), channel_id=1, source_target_pairs={{0,32},{32,0},{64,96},{96,64},{128,160},{160,128},{192,224},{224,1... | collective-permute-start | bytes 1769480 | tf_op jit(solution)/shard_map/ppermute | solution.py:101
  87.5 4.4 %collective-permute-start.2 = (bf16[384,768]{1,0:T(8,128)(2,1)}, bf16[384,768]{1,0:T(8,128)(2,1)}, u32[]{:S(2)}, u32[]{:S(2)}) collective-permute-start(bf16[384,768]{1,0:T(8,128)(2,1)} %collective-permute-done.1), channel_id=1, source_target_pairs={{0,32},{32,0},{64,96},{96,64},{128,160},{160,128},{192,224},{224,1... | collective-permute-start | bytes 1769480 | tf_op jit(solution)/shard_map/ppermute | solution.py:101
  96.9 24.9 %all-to-all-start.2 = ((bf16[32,16,768]{2,1,0:T(8,128)(2,1)}), bf16[32,16,768]{2,1,0:T(8,128)(2,1)S(1)}, u32[]{:S(2)}, u32[]{:S(2)}) async-start(bf16[32,16,768]{2,1,0:T(8,128)(2,1)} %shard_map.50), calls=%async_computation.2 | async-start | bytes 1572864 | tf_op jit(solution)/shard_map/all_to_all | solution.py:150
  104.6 29.1 %collective-permute-start.4 = (bf16[384,768]{1,0:T(8,128)(2,1)}, bf16[384,768]{1,0:T(8,128)(2,1)}, u32[]{:S(2)}, u32[]{:S(2)}) collective-permute-start(bf16[384,768]{1,0:T(8,128)(2,1)} %fusion.3), channel_id=1, source_target_pairs={{0,4},{4,0},{8,12},{12,8},{16,20},{20,16},{24,28},{28,24},{1,5},{5... | collective-permute-start | bytes 1769480 | tf_op jit(solution)/shard_map/ppermute | solution.py:105

commit v2 on v0

v2 whole, which is shorter than its diff:
```python
import jax
import jax.numpy as jnp
from jax import lax
from jax.experimental import pallas as pl
from jax.experimental.pallas import tpu as pltpu
from jax.sharding import PartitionSpec as P

NX, NZ, NC, NY = 4, 2, 4, 8
T, F, B = 16, 768, 384


def depth_of(zl, x, core):
    return (zl * NX + x) * 2 + core


def x_groups():
    return [[depth_of(zl, x, core) for x in range(NX)] for zl in range(NZ) for core in range(2)]


def token_groups():
    return [
        [
            depth_of(zl, x, core) * NY + 2 * y4 + parity
            for x in range(NX)
            for core in range(2)
            for y4 in range(NY // 2)
        ]
        for zl in range(NZ)
        for parity in range(2)
    ]


def exchange(x, axes, groups=None):
    return lax.all_to_all(
        x, axes, split_axis=0, concat_axis=0, axis_index_groups=groups, tiled=True
    )


def call(kernel, out_shape, scalars, *operands):
    n = len(operands)
    return pl.pallas_call(
        kernel,
        out_shape=out_shape,
        in_specs=[pl.BlockSpec(memory_space=pltpu.SMEM)]
        + [pl.BlockSpec(memory_space=pltpu.VMEM)] * n,
        out_specs=jax.tree.map(lambda _: pl.BlockSpec(memory_space=pltpu.VMEM), out_shape),
        compiler_params=pltpu.CompilerParams(vmem_limit_bytes=48 * 1024 * 1024),
    )(scalars, *operands)


def spread_kernel(s_ref, x_ref, o_ref):
    for x in range(NX):
        for core in range(2):
            for zl in range(NZ):
                block = x_ref[:, pl.ds(depth_of(zl, x, core) * B, B)]
                for y4 in range(NY // 2):
                    o_ref[x, core, y4, :, pl.ds(zl * B, B)] = block


def block_at(zl):
    return pl.ds(pl.multiple_of(zl * B, B), B)


def rows_at(g_ref, parity):
    return g_ref[:, :, parity].reshape(NX * NY // 2 * T, F)


def terms_kernel(other, s_ref, g_ref, h_ref, w_ref, v_ref, o_ref):
    zl, core, parity = s_ref[0], s_ref[1], s_ref[2]
    at = 1 - parity if other else parity
    g = jnp.concatenate([rows_at(g_ref, at), rows_at(h_ref, at)], axis=0)
    for w, z in ((w_ref, zl), (v_ref, 1 - zl)):
        total = lax.dot_general(
            g, w[...], (((1,), (1,)), ((), ())), preferred_element_type=jnp.float32
        ).astype(jnp.bfloat16)
        total = total.reshape(2, NX, NY // 2, T, B)
        o_ref[:, core, :, :, block_at(z)] = total[0]
        o_ref[:, 1 - core, :, :, block_at(z)] = total[1]


def weight_product(s_ref, mine_ref, theirs_ref, g_ref, h_ref, flip_z):
    zl, core, parity = s_ref[0], s_ref[1], s_ref[2]
    at = block_at(1 - zl if flip_z else zl)
    acts = jnp.concatenate(
        [
            a[:, c, :, :, at].reshape(NX * NY // 2 * T, B)
            for c in (core, 1 - core)
            for a in (mine_ref, theirs_ref)
        ],
        axis=0,
    )
    grads = jnp.concatenate(
        [rows_at(g, p) for g in (g_ref, h_ref) for p in (parity, 1 - parity)], axis=0
    )
    return lax.dot_general(
        acts, grads, (((0,), (0,)), ((), ())), preferred_element_type=jnp.float32
    )


def weight_kernel(flip, s_ref, mine_ref, theirs_ref, g_ref, h_ref, o_ref):
    o_ref[...] = weight_product(s_ref, mine_ref, theirs_ref, g_ref, h_ref, flip).astype(o_ref.dtype)


def add_kernel(s_ref, a_ref, b_ref, o_ref):
    for i in range(NX * NY):
        o_ref[i] = a_ref[i] + b_ref[i]


def last_kernel(s_ref, a_ref, b_ref, o_ref):
    o_ref[...] = (a_ref[...] + b_ref[...].astype(jnp.float32)).astype(o_ref.dtype)


def sum_kernel(s_ref, x_ref, o_ref):
    for x in range(NX):
        for core in range(2):
            total = x_ref[x, core, 0].astype(jnp.float32)
            for y4 in range(1, NY // 2):
                total = total + x_ref[x, core, y4].astype(jnp.float32)
            for zl in range(NZ):
                o_ref[:, pl.ds(depth_of(zl, x, core) * B, B)] = total[:, zl * B : zl * B + B].astype(
                    jnp.bfloat16
                )


def swap_core(x):
    return lax.ppermute(x, "depth", [(i, i ^ 1) for i in range(16)])


def swap_z(x):
    return lax.ppermute(x, "depth", [(i, i ^ 8) for i in range(16)])


def swap_row(x):
    pairs = []
    for d in range(16):
        for y in range(NY):
            step = 1 if y % 2 == d % 2 else NY - 1
            pairs.append((d * NY + y, d * NY + (y + step) % NY))
    return lax.ppermute(x, ("depth", "row"), pairs)


def local(inputs, grad_out, weight):
    bf, f32 = jnp.bfloat16, jnp.float32
    shape = jax.ShapeDtypeStruct
    depth, row = lax.axis_index("depth"), lax.axis_index("row")
    s = jnp.stack([depth // 8, depth % 2, row % 2]).astype(jnp.int32)
    w = weight.reshape(B, F)
    half = shape((NX, 2, NY // 2, T, 2 * B), bf)
    flat = (NX * NY, T, 2 * B)

    spread = call(spread_kernel, half, s, inputs)
    mine = exchange(spread.reshape(flat), ("depth", "row"), token_groups())
    slab = lax.all_gather(grad_out, "col", axis=0, tiled=True)
    slab, w = lax.optimization_barrier((slab, w))
    w_z = swap_z(w)
    grads = lax.all_gather(slab, "depth", axis=0, tiled=True, axis_index_groups=x_groups())
    mine, grads, w_z = lax.optimization_barrier((mine, grads, w_z))
    others = swap_core(grads)
    theirs = swap_row(mine)
    grads = grads.reshape(NX, NY // 2, 2, T, F)
    others = others.reshape(NX, NY // 2, 2, T, F)

    def terms(other):
        return call(
            lambda *refs: terms_kernel(other, *refs), half, s, grads, others, w, w_z
        ).reshape(flat)

    sent = terms(True)
    got = swap_row(sent)
    theirs, sent = lax.optimization_barrier((theirs, sent))

    def weight_term(flip, dtype):
        return call(
            lambda *refs: weight_kernel(flip, *refs),
            shape((B, F), dtype),
            s,
            mine.reshape(half.shape),
            theirs.reshape(half.shape),
            grads,
            others,
        )

    far, keep = weight_term(True, bf), terms(False)
    got, far, keep = lax.optimization_barrier((got, far, keep))
    part = call(add_kernel, shape(flat, bf), s, keep, got)
    summed = exchange(part, ("depth", "row"), token_groups())
    grad_inputs = call(sum_kernel, shape((T, 16 * B), bf), s, summed.reshape(half.shape))
    grad_weight = call(last_kernel, shape((B, F), bf), s, weight_term(False, f32), swap_z(far))
    return grad_inputs, grad_weight.reshape(weight.shape)


def solution(mesh):
    in_specs = (P(("depth", "row"), "col"), P(("depth", "col"), "row"), P("col", "depth", "row"))
    out_specs = (P(("depth", "row"), "col"), P("col", "depth", "row"))
    return jax.shard_map(local, mesh=mesh, in_specs=in_specs, out_specs=out_specs, check_vma=False)
```

time: 226 us -> 111 us (0.49); the launches traced: 223 us -> 111 us
  waiting for transfers between devices: 163 us -> 27.7 us
  starting transfers between devices: 10.4 us -> 38.3 us
  between operations: 13.8 us -> 0.79 us
  matrix products: 12.1 us -> 0 us
  Pallas kernels: 0 us -> 11.6 us
  blocking collectives: 19.5 us -> 29.5 us
    all_gather x3 -> x0, waiting for transfers between devices: 124 us -> none  [the longest x1 65.8 us: local(): tile_full = lax.all_gather(weight, 'depth', axis=1, tiled=True)[0]]
    reduce_scatter x1 -> x0, waiting for transfers between devices: 37.7 us -> none  [local(): lax.psum_scatter(round_term(lax.dot_general(slab_rows, tile_full, (((1,),...]
    ppermute x0 -> x5, waiting for transfers between devices: none -> 22.9 us  [the longest x2 12.3 us: swap_z(): return lax.ppermute(x, 'depth', [(i, i ^ 8) for i in range(16)])]
    ppermute x0 -> x5, starting transfers between devices: none -> 19.3 us  [the longest x1 7.74 us: swap_core(): return lax.ppermute(x, 'depth', [(i, i ^ 1) for i in range(16)])]
    dot_general x2 -> x0, matrix products: 12.1 us -> none  [the longest x1 7.98 us: local(): lax.dot_general(slab_rows, tile_full, (((1,), (1,)), ((), ())), preferred...]
    pallas_call x0 -> x8, Pallas kernels: none -> 11.6 us  [call(): pl.pallas_call(kernel, out_shape=out_shape, in_specs=[pl.BlockSpec(memory...]
    all_gather x1 -> x2, blocking collectives: 19.5 us -> 29.5 us  [the longest x1 17.6 us: local(): slab = lax.all_gather(grad_out, 'col', axis=0, tiled=True)]
    all_to_all x1 -> x2, starting transfers between devices: 10.2 us -> 19.1 us  [exchange(): lax.all_to_all(x, axes, split_axis=0, concat_axis=0, axis_index_groups=gr...]
  transfers between devices with their start and end apart: 5 -> 7, of which waited for: 4 -> 4; matrix products, arithmetic and copies ran while one was open for 7% -> 0% of each run, Pallas kernels for 0% -> 7%
where the time goes in v2:
time: 111 us
  starting transfers between devices  38.3 us (35%)
  blocking collectives  29.5 us (27%)
  waiting for transfers between devices  27.7 us (25%)
  Pallas kernels  11.6 us (10%)
  local copies, waits for them, and re-layouts  2.88 us (3%)
    all_to_all x2, starting transfers between devices, exchange(): lax.all_to_all(x, axes, split_axis=0, concat_axis=0, axis_index_groups=gr...  19.1 us
    all_gather x1, blocking collectives, local(): slab = lax.all_gather(grad_out, 'col', axis=0, tiled=True)  17.6 us
    ppermute x2, waiting for transfers between devices, swap_z(): return lax.ppermute(x, 'depth', [(i, i ^ 8) for i in range(16)])  12.3 us
    all_gather x1, blocking collectives, local(): lax.all_gather(slab, 'depth', axis=0, tiled=True, axis_index_groups=x_gro...  11.9 us
    pallas_call x8, Pallas kernels, call(): pl.pallas_call(kernel, out_shape=out_shape, in_specs=[pl.BlockSpec(memory...  11.6 us
    ppermute x2, waiting for transfers between devices, swap_row(): return lax.ppermute(x, ('depth', 'row'), pairs)  10.6 us
    ppermute x1, starting transfers between devices, swap_core(): return lax.ppermute(x, 'depth', [(i, i ^ 1) for i in range(16)])  7.74 us
    ppermute x2, starting transfers between devices, swap_row(): return lax.ppermute(x, ('depth', 'row'), pairs)  6.49 us
  transfers between devices with their start and end apart: 7, of which 4 were waited for; matrix products, arithmetic and copies ran while one was open for 0% of the time, Pallas kernels for 7%

profile of v2, /device:TPU:1, one launch (start us, length us, event | category | flops | bytes accessed | tf_op | source)
XLA Modules:
  0.0 111.0 jit_solution(16079326704790057293)
XLA Ops:
  0.7 0.1 pad_add_fusion.s_ref.refs_0_
  0.7 0.0 copy-start.4
  0.7 0.9 copy-done.4
  1.7 0.0 copy-start.5
  1.7 0.0 copy-start.2
  1.7 1.5 %shard_map.50 = bf16[4,2,4,16,768]{4,3,2,1,0:T(8,128)(2,1)} custom-call(s32[3]{0:T(128)S(1)} %pad_add_fusion.s_ref.refs_0_, bf16[16,6144]{1,0:T(8,128)(2,1)S(1)} %copy-done.4), custom_call_target="tpu_custom_call" | custom-call | tf_op jit(solution)/shard_map/pallas_call | solution.py:41
  3.2 11.2 %all-to-all-start = ((bf16[32,16,768]{2,1,0:T(8,128)(2,1)}), bf16[32,16,768]{2,1,0:T(8,128)(2,1)S(1)}, u32[]{:S(2)}, u32[]{:S(2)}) async-start(bf16[32,16,768]{2,1,0:T(8,128)(2,1)} %bitcast.3), calls=%async_computation | async-start | bytes 1572864 | tf_op jit(solution)/shard_map/all_to_all | solution.py:34
  14.4 0.0 copy-done.5
  14.4 17.6 %all_gather.6 = bf16[128,768]{1,0:T(8,128)(2,1)S(1)} all-gather(bf16[32,768]{1,0:T(8,128)(2,1)S(1)} %copy-done.5), channel_id=1, replica_groups=mesh['depth'=16,'row'=8,'col'=4] {'col'}, dimensions={0}, use_global_device_ids=true | all-gather | bytes 245760 | tf_op jit(solution)/shard_map/all_gather | solution.py:153
  32.0 0.0 copy-done.2
  32.0 3.1 %collective-permute-start = (bf16[384,768]{1,0:T(8,128)(2,1)S(1)}, bf16[384,768]{1,0:T(8,128)(2,1)S(1)}, u32[]{:S(2)}, u32[]{:S(2)}) collective-permute-start(bf16[384,768]{1,0:T(8,128)(2,1)S(1)} %bitcast.27), channel_id=1, source_target_pairs={{0,256},{32,288},{64,320},{96,352},{128,384},{160,416},{192,448},{... | collective-permute-start | bytes 1769480 | tf_op jit(solution)/shard_map/ppermute | solution.py:130
  35.1 11.9 %all_gather.7 = bf16[512,768]{1,0:T(8,128)(2,1)S(1)} all-gather(bf16[128,768]{1,0:T(8,128)(2,1)S(1)} %all_gather.6), channel_id=1, replica_groups={{0,64,128,192},{32,96,160,224},{256,320,384,448},{288,352,416,480},{1,6..., dimensions={0}, use_global_device_ids=true | all-gather | bytes 983040 | tf_op jit(solution)/shard_map/all_gather | solution.py:156
  47.0 0.0 collective-permute-done.refs_4_
  47.0 0.0 all-to-all-done
  47.0 7.7 %collective-permute-start.1 = (bf16[512,768]{1,0:T(8,128)(2,1)S(1)}, bf16[512,768]{1,0:T(8,128)(2,1)S(1)}, u32[]{:S(2)}, u32[]{:S(2)}) collective-permute-start(bf16[512,768]{1,0:T(8,128)(2,1)S(1)} %all_gather.7), channel_id=1, source_target_pairs={{0,32},{32,0},{64,96},{96,64},{128,160},{160,128},{192,224},{224,1... | collective-permute-start | bytes 2359304 | tf_op jit(solution)/shard_map/ppermute | solution.py:126
  54.8 4.4 %collective-permute-start.3 = (bf16[32,16,768]{2,1,0:T(8,128)(2,1)S(1)}, bf16[32,16,768]{2,1,0:T(8,128)(2,1)S(1)}, u32[]{:S(2)}, u32[]{:S(2)}) collective-permute-start(bf16[32,16,768]{2,1,0:T(8,128)(2,1)S(1)} %all-to-all-done), channel_id=1, source_target_pairs={{0,4},{4,0},{8,12},{12,8},{16,20},{20,16},{24,28},{28,24},{32,60},... | collective-permute-start | bytes 2359304 | tf_op jit(solution)/shard_map/ppermute | solution.py:139
  59.2 0.0 collective-permute-done.1
  59.2 1.5 %shard_map.51 = bf16[4,2,4,16,768]{4,3,2,1,0:T(8,128)(2,1)S(1)} custom-call(s32[3]{0:T(128)S(1)} %pad_add_fusion.s_ref.refs_0_, bf16[4,4,2,16,768]{4,3,2,1,0:T(8,128)(2,1)S(1)} %bitcast.13, bf16[4,4,2,16,768]{4,3,2,1,0:T(8,128)(2,1)S(1)} %bitcast.17, bf16[384,768]{1,0:T(8,128)(2,1)S(1)} %bitcast.28, bf16[384,768]{1,0:T(8,128)(2,1)S(1)} %collective-permute-done.refs_4_), custom_call_target="tpu_custom_call" | custom-call | tf_op jit(solution)/shard_map/pallas_call | solution.py:41
  60.7 2.1 %collective-permute-start.2 = (bf16[32,16,768]{2,1,0:T(8,128)(2,1)S(1)}, bf16[32,16,768]{2,1,0:T(8,128)(2,1)S(1)}, u32[]{:S(2)}, u32[]{:S(2)}) collective-permute-start(bf16[32,16,768]{2,1,0:T(8,128)(2,1)S(1)} %bitcast.30), channel_id=1, source_target_pairs={{0,4},{4,0},{8,12},{12,8},{16,20},{20,16},{24,28},{28,24},{32,60},... | collective-permute-start | bytes 2359304 | tf_op jit(solution)/shard_map/ppermute | solution.py:139
  62.8 1.5 %shard_map.53 = bf16[4,2,4,16,768]{4,3,2,1,0:T(8,128)(2,1)S(1)} custom-call(s32[3]{0:T(128)S(1)} %pad_add_fusion.s_ref.refs_0_, bf16[4,4,2,16,768]{4,3,2,1,0:T(8,128)(2,1)S(1)} %bitcast.14, bf16[4,4,2,16,768]{4,3,2,1,0:T(8,128)(2,1)S(1)} %bitcast.18, bf16[384,768]{1,0:T(8,128)(2,1)S(1)} %bitcast.29, bf16[384,768]{1,0:T(8,128)(2,1)S(1)} %collective-permute-done.refs_4_), custom_call_target="tpu_custom_call" | custom-call | tf_op jit(solution)/shard_map/pallas_call | solution.py:41
  64.4 4.4 %collective-permute-done.3 = bf16[32,16,768]{2,1,0:T(8,128)(2,1)S(1)} collective-permute-done((bf16[32,16,768]{2,1,0:T(8,128)(2,1)S(1)}, bf16[32,16,768]{2,1,0:T(8,128)(2,1)S(1)}, u32[]{:S(2)}, u32[]{:S(2)}) %collective-permute-start.3) | collective-permute-done | bytes 786464 | tf_op jit(solution)/shard_map/ppermute | solution.py:139
  68.7 0.0 copy-start
  68.7 1.4 %shard_map.52 = bf16[384,768]{1,0:T(8,128)(2,1)S(1)} custom-call(s32[3]{0:T(128)S(1)} %pad_add_fusion.s_ref.refs_0_, bf16[4,2,4,16,768]{4,3,2,1,0:T(8,128)(2,1)S(1)} %bitcast.21, bf16[4,2,4,16,768]{4,3,2,1,0:T(8,128)(2,1)S(1)} %bitcast.24, bf16[4,4,2,16,768]{4,3,2,1,0:T(8,128)(2,1)S(1)} %bitcast.15, bf16[4,4,2,16,768]{4,3,2,1,0:T(8,128)(2,1)S(1)} %bitcast.19), custom_call_target="tpu_custom_call" | custom-call | tf_op jit(solution)/shard_map/pallas_call | solution.py:41
  70.1 0.0 copy-done
  70.1 0.0 copy-start.3
  70.2 0.8 copy-done.3
  71.0 6.2 %collective-permute-done.2.b_ref = bf16[32,16,768]{2,1,0:T(8,128)(2,1)S(1)} collective-permute-done((bf16[32,16,768]{2,1,0:T(8,128)(2,1)S(1)}, bf16[32,16,768]{2,1,0:T(8,128)(2,1)S(1)}, u32[]{:S(2)}, u32[]{:S(2)}) %collective-permute-start.2) | collective-permute-done | bytes 786464 | tf_op jit(solution)/shard_map/ppermute | solution.py:139
  77.2 1.5 %shard_map.54 = bf16[32,16,768]{2,1,0:T(8,128)(2,1)} custom-call(s32[3]{0:T(128)S(1)} %pad_add_fusion.s_ref.refs_0_, bf16[32,16,768]{2,1,0:T(8,128)(2,1)S(1)} %bitcast.26, bf16[32,16,768]{2,1,0:T(8,128)(2,1)S(1)} %collective-permute-done.2.b_ref), custom_call_target="tpu_custom_call" | custom-call | tf_op jit(solution)/shard_map/pallas_call | solution.py:41
  78.7 7.9 %all-to-all-start.1 = ((bf16[32,16,768]{2,1,0:T(8,128)(2,1)}), bf16[32,16,768]{2,1,0:T(8,128)(2,1)S(1)}, u32[]{:S(2)}, u32[]{:S(2)}) async-start(bf16[32,16,768]{2,1,0:T(8,128)(2,1)} %shard_map.54), calls=%async_computation.1 | async-start | bytes 1572864 | tf_op jit(solution)/shard_map/all_to_all | solution.py:34
  86.6 1.9 %collective-permute-start.4 = (bf16[384,768]{1,0:T(8,128)(2,1)}, bf16[384,768]{1,0:T(8,128)(2,1)S(1)}, u32[]{:S(2)}, u32[]{:S(2)}) collective-permute-start(bf16[384,768]{1,0:T(8,128)(2,1)} %copy-done.3), channel_id=1, source_target_pairs={{0,256},{32,288},{64,320},{96,352},{128,384},{160,416},{192,448},{... | collective-permute-start | bytes 1769480 | tf_op jit(solution)/shard_map/ppermute | solution.py:130
  88.5 0.0 copy-start.1
  88.5 1.1 %copy-done.1 = bf16[32,16,768]{2,1,0:T(8,128)(2,1)S(1)} copy-done((bf16[32,16,768]{2,1,0:T(8,128)(2,1)S(1)}, bf16[32,16,768]{2,1,0:T(8,128)(2,1)}, u32[]{:S(2)}) %copy-start.1) | copy-done | bytes 786456
  89.7 1.4 %shard_map.56.a_ref = f32[384,768]{1,0:T(8,128)S(1)} custom-call(s32[3]{0:T(128)S(1)} %pad_add_fusion.s_ref.refs_0_, bf16[4,2,4,16,768]{4,3,2,1,0:T(8,128)(2,1)S(1)} %bitcast.22, bf16[4,2,4,16,768]{4,3,2,1,0:T(8,128)(2,1)S(1)} %bitcast.25, bf16[4,4,2,16,768]{4,3,2,1,0:T(8,128)(2,1)S(1)} %bitcast.16, bf16[4,4,2,16,768]{4,3,2,1,0:T(8,128)(2,1)S(1)} %bitcast.20), custom_call_target="tpu_custom_call" | custom-call | tf_op jit(solution)/shard_map/pallas_call | solution.py:41
  91.0 12.3 %collective-permute-done.4.b_ref = bf16[384,768]{1,0:T(8,128)(2,1)S(1)} collective-permute-done((bf16[384,768]{1,0:T(8,128)(2,1)}, bf16[384,768]{1,0:T(8,128)(2,1)S(1)}, u32[]{:S(2)}, u32[]{:S(2)}) %collective-permute-start.4) | collective-permute-done | bytes 589856 | tf_op jit(solution)/shard_map/ppermute | solution.py:130
  103.4 1.5 %shard_map.57 = bf16[384,768]{1,0:T(8,128)(2,1)} custom-call(s32[3]{0:T(128)S(1)} %pad_add_fusion.s_ref.refs_0_, f32[384,768]{1,0:T(8,128)S(1)} %shard_map.56.a_ref, bf16[384,768]{1,0:T(8,128)(2,1)S(1)} %collective-permute-done.4.b_ref), custom_call_target="tpu_custom_call" | custom-call | tf_op jit(solution)/shard_map/pallas_call | solution.py:41
  104.8 4.8 %all-to-all-done.1 = bf16[32,16,768]{2,1,0:T(8,128)(2,1)S(1)} async-done(((bf16[32,16,768]{2,1,0:T(8,128)(2,1)}), bf16[32,16,768]{2,1,0:T(8,128)(2,1)S(1)}, u32[]{:S(2)}, u32[]{:S(2)}) %all-to-all-start.1) | async-done | bytes 786464 | tf_op jit(solution)/shard_map/all_to_all | solution.py:34
  109.6 1.3 %shard_map.55 = bf16[16,6144]{1,0:T(8,128)(2,1)} custom-call(s32[3]{0:T(128)S(1)} %pad_add_fusion.s_ref.refs_0_, bf16[4,2,4,16,768]{4,3,2,1,0:T(8,128)(2,1)S(1)} %bitcast.23), custom_call_target="tpu_custom_call" | custom-call | tf_op jit(solution)/shard_map/pallas_call | solution.py:41
Async XLA Ops:
  0.7 0.9 copy-start.4
  1.7 12.8 %copy-start.5 = (bf16[32,768]{1,0:T(8,128)(2,1)S(1)}, bf16[32,768]{1,0:T(8,128)(2,1)}, u32[]{:S(2)}) copy-start(bf16[32,768]{1,0:T(8,128)(2,1)} %param.4) | copy-start | bytes 147460
  1.7 30.4 %copy-start.2 = (bf16[1,384,768]{2,1,0:T(8,128)(2,1)S(1)}, bf16[1,384,768]{2,1,0:T(8,128)(2,1)}, u32[]{:S(2)}) copy-start(bf16[1,384,768]{2,1,0:T(8,128)(2,1)} %param.5) | copy-start | bytes 1769476
  3.2 43.9 %all-to-all-start = ((bf16[32,16,768]{2,1,0:T(8,128)(2,1)}), bf16[32,16,768]{2,1,0:T(8,128)(2,1)S(1)}, u32[]{:S(2)}, u32[]{:S(2)}) async-start(bf16[32,16,768]{2,1,0:T(8,128)(2,1)} %bitcast.3), calls=%async_computation | async-start | bytes 1572864 | tf_op jit(solution)/shard_map/all_to_all | solution.py:34
  32.0 15.0 %collective-permute-start = (bf16[384,768]{1,0:T(8,128)(2,1)S(1)}, bf16[384,768]{1,0:T(8,128)(2,1)S(1)}, u32[]{:S(2)}, u32[]{:S(2)}) collective-permute-start(bf16[384,768]{1,0:T(8,128)(2,1)S(1)} %bitcast.27), channel_id=1, source_target_pairs={{0,256},{32,288},{64,320},{96,352},{128,384},{160,416},{192,448},{... | collective-permute-start | bytes 1769480 | tf_op jit(solution)/shard_map/ppermute | solution.py:130
  47.0 12.1 %collective-permute-start.1 = (bf16[512,768]{1,0:T(8,128)(2,1)S(1)}, bf16[512,768]{1,0:T(8,128)(2,1)S(1)}, u32[]{:S(2)}, u32[]{:S(2)}) collective-permute-start(bf16[512,768]{1,0:T(8,128)(2,1)S(1)} %all_gather.7), channel_id=1, source_target_pairs={{0,32},{32,0},{64,96},{96,64},{128,160},{160,128},{192,224},{224,1... | collective-permute-start | bytes 2359304 | tf_op jit(solution)/shard_map/ppermute | solution.py:126
  54.8 13.9 %collective-permute-start.3 = (bf16[32,16,768]{2,1,0:T(8,128)(2,1)S(1)}, bf16[32,16,768]{2,1,0:T(8,128)(2,1)S(1)}, u32[]{:S(2)}, u32[]{:S(2)}) collective-permute-start(bf16[32,16,768]{2,1,0:T(8,128)(2,1)S(1)} %all-to-all-done), channel_id=1, source_target_pairs={{0,4},{4,0},{8,12},{12,8},{16,20},{20,16},{24,28},{28,24},{32,60},... | collective-permute-start | bytes 2359304 | tf_op jit(solution)/shard_map/ppermute | solution.py:139
  60.7 16.5 %collective-permute-start.2 = (bf16[32,16,768]{2,1,0:T(8,128)(2,1)S(1)}, bf16[32,16,768]{2,1,0:T(8,128)(2,1)S(1)}, u32[]{:S(2)}, u32[]{:S(2)}) collective-permute-start(bf16[32,16,768]{2,1,0:T(8,128)(2,1)S(1)} %bitcast.30), channel_id=1, source_target_pairs={{0,4},{4,0},{8,12},{12,8},{16,20},{20,16},{24,28},{28,24},{32,60},... | collective-permute-start | bytes 2359304 | tf_op jit(solution)/shard_map/ppermute | solution.py:139
  68.7 1.4 %copy-start = (bf16[32,16,768]{2,1,0:T(8,128)(2,1)}, bf16[32,16,768]{2,1,0:T(8,128)(2,1)S(1)}, u32[]{:S(2)}) copy-start(bf16[32,16,768]{2,1,0:T(8,128)(2,1)S(1)} %collective-permute-done.3) | copy-start | bytes 2359300
  70.1 0.8 copy-start.3
  78.7 30.9 %all-to-all-start.1 = ((bf16[32,16,768]{2,1,0:T(8,128)(2,1)}), bf16[32,16,768]{2,1,0:T(8,128)(2,1)S(1)}, u32[]{:S(2)}, u32[]{:S(2)}) async-start(bf16[32,16,768]{2,1,0:T(8,128)(2,1)} %shard_map.54), calls=%async_computation.1 | async-start | bytes 1572864 | tf_op jit(solution)/shard_map/all_to_all | solution.py:34
  86.6 16.8 %collective-permute-start.4 = (bf16[384,768]{1,0:T(8,128)(2,1)}, bf16[384,768]{1,0:T(8,128)(2,1)S(1)}, u32[]{:S(2)}, u32[]{:S(2)}) collective-permute-start(bf16[384,768]{1,0:T(8,128)(2,1)} %copy-done.3), channel_id=1, source_target_pairs={{0,256},{32,288},{64,320},{96,352},{128,384},{160,416},{192,448},{... | collective-permute-start | bytes 1769480 | tf_op jit(solution)/shard_map/ppermute | solution.py:130
  88.5 1.1 %copy-start.1 = (bf16[32,16,768]{2,1,0:T(8,128)(2,1)S(1)}, bf16[32,16,768]{2,1,0:T(8,128)(2,1)}, u32[]{:S(2)}) copy-start(bf16[32,16,768]{2,1,0:T(8,128)(2,1)} %copy-done) | copy-start | bytes 2359300

commit v3 on v2

--- a/solution.py
+++ b/solution.py
@@ -36,7 +36,7 @@
     )
 
 
-def call(kernel, out_shape, scalars, *operands):
+def call(kernel, out_shape, scalars, *operands, cost=None):
     n = len(operands)
     return pl.pallas_call(
         kernel,
@@ -45,6 +45,7 @@
         + [pl.BlockSpec(memory_space=pltpu.VMEM)] * n,
         out_specs=jax.tree.map(lambda _: pl.BlockSpec(memory_space=pltpu.VMEM), out_shape),
         compiler_params=pltpu.CompilerParams(vmem_limit_bytes=48 * 1024 * 1024),
+        cost_estimate=cost and pl.CostEstimate(flops=cost, bytes_accessed=0, transcendentals=0),
     )(scalars, *operands)
 
 
@@ -156,7 +157,6 @@
     grads = lax.all_gather(slab, "depth", axis=0, tiled=True, axis_index_groups=x_groups())
     mine, grads, w_z = lax.optimization_barrier((mine, grads, w_z))
     others = swap_core(grads)
-    theirs = swap_row(mine)
     grads = grads.reshape(NX, NY // 2, 2, T, F)
     others = others.reshape(NX, NY // 2, 2, T, F)
 
@@ -167,9 +167,10 @@
 
     sent = terms(True)
     got = swap_row(sent)
-    theirs, sent = lax.optimization_barrier((theirs, sent))
+    mine, sent = lax.optimization_barrier((mine, sent))
+    theirs = swap_row(mine)
 
-    def weight_term(flip, dtype):
+    def weight_term(flip, dtype, cost=None):
         return call(
             lambda *refs: weight_kernel(flip, *refs),
             shape((B, F), dtype),
@@ -178,14 +179,14 @@
             theirs.reshape(half.shape),
             grads,
             others,
+            cost=cost,
         )
 
-    far, keep = weight_term(True, bf), terms(False)
-    got, far, keep = lax.optimization_barrier((got, far, keep))
-    part = call(add_kernel, shape(flat, bf), s, keep, got)
+    part = call(add_kernel, shape(flat, bf), s, terms(False), got)
     summed = exchange(part, ("depth", "row"), token_groups())
     grad_inputs = call(sum_kernel, shape((T, 16 * B), bf), s, summed.reshape(half.shape))
-    grad_weight = call(last_kernel, shape((B, F), bf), s, weight_term(False, f32), swap_z(far))
+    crossed = swap_z(weight_term(True, bf, 10**10))
+    grad_weight = call(last_kernel, shape((B, F), bf), s, weight_term(False, f32), crossed)
     return grad_inputs, grad_weight.reshape(weight.shape)
 
 

time: 111 us -> 107 us (0.964)
  waiting for transfers between devices: 27.7 us -> 23.4 us
  local copies, waits for them, and re-layouts: 2.88 us -> 0.94 us
  Pallas kernels: 11.6 us -> 12.8 us
    ppermute x2, waiting for transfers between devices: 10.6 us -> 5.91 us  [swap_row(): return lax.ppermute(x, ('depth', 'row'), pairs)]
    unnamed x12 -> x6, local copies, waits for them, and re-layouts: 2.88 us -> 0.94 us
    all_to_all x2, waiting for transfers between devices: 4.81 us -> 2.89 us  [exchange(): lax.all_to_all(x, axes, split_axis=0, concat_axis=0, axis_index_groups=gr...]
    ppermute x1, waiting for transfers between devices: 0.01 us -> 1.89 us  [swap_core(): return lax.ppermute(x, 'depth', [(i, i ^ 1) for i in range(16)])]
    pallas_call x8, Pallas kernels: 11.6 us -> 12.8 us  [call(): pl.pallas_call(kernel, out_shape=out_shape, in_specs=[pl.BlockSpec(memory...]
  transfers between devices with their start and end apart: 7 -> 7, of which waited for: 4 -> 4; matrix products, arithmetic and copies ran while one was open for 0% -> 0% of each run, Pallas kernels for 7% -> 8%
where the time goes in v3:
time: 107 us; the launch traced here: 106 us
  starting transfers between devices  38.5 us (36%)
  blocking collectives  29.5 us (28%)
  waiting for transfers between devices  23.4 us (22%)
  Pallas kernels  12.8 us (12%)
    all_to_all x2, starting transfers between devices, exchange(): lax.all_to_all(x, axes, split_axis=0, concat_axis=0, axis_index_groups=gr...  19.3 us
    all_gather x1, blocking collectives, local(): slab = lax.all_gather(grad_out, 'col', axis=0, tiled=True)  17.6 us
    pallas_call x8, Pallas kernels, call(): pl.pallas_call(kernel, out_shape=out_shape, in_specs=[pl.BlockSpec(memory...  12.8 us
    ppermute x2, waiting for transfers between devices, swap_z(): return lax.ppermute(x, 'depth', [(i, i ^ 8) for i in range(16)])  12.7 us
    all_gather x1, blocking collectives, local(): lax.all_gather(slab, 'depth', axis=0, tiled=True, axis_index_groups=x_gro...  11.9 us
    ppermute x1, starting transfers between devices, swap_core(): return lax.ppermute(x, 'depth', [(i, i ^ 1) for i in range(16)])  7.74 us
    ppermute x2, starting transfers between devices, swap_row(): return lax.ppermute(x, ('depth', 'row'), pairs)  6.49 us
    ppermute x2, waiting for transfers between devices, swap_row(): return lax.ppermute(x, ('depth', 'row'), pairs)  5.91 us
  transfers between devices with their start and end apart: 7, of which 4 were waited for; matrix products, arithmetic and copies ran while one was open for 0% of the time, Pallas kernels for 8%

profile of v3, /device:TPU:1, one launch (start us, length us, event | category | flops | bytes accessed | tf_op | source)
XLA Modules:
  0.0 106.0 jit_solution(7762438048547313004)
XLA Ops:
  0.7 0.1 pad_add_fusion.s_ref.refs_0_
  0.7 0.0 copy-start.1
  0.7 0.9 copy-done.1
  1.7 0.0 copy-start.2
  1.7 0.0 copy-start
  1.7 1.5 %shard_map.50 = bf16[4,2,4,16,768]{4,3,2,1,0:T(8,128)(2,1)} custom-call(s32[3]{0:T(128)S(1)} %pad_add_fusion.s_ref.refs_0_, bf16[16,6144]{1,0:T(8,128)(2,1)S(1)} %copy-done.1), custom_call_target="tpu_custom_call" | custom-call | tf_op jit(solution)/shard_map/pallas_call | solution.py:41
  3.2 11.2 %all-to-all-start = ((bf16[32,16,768]{2,1,0:T(8,128)(2,1)}), bf16[32,16,768]{2,1,0:T(8,128)(2,1)S(1)}, u32[]{:S(2)}, u32[]{:S(2)}) async-start(bf16[32,16,768]{2,1,0:T(8,128)(2,1)} %bitcast.3), calls=%async_computation | async-start | bytes 1572864 | tf_op jit(solution)/shard_map/all_to_all | solution.py:34
  14.4 0.0 copy-done.2
  14.4 17.6 %all_gather.6 = bf16[128,768]{1,0:T(8,128)(2,1)S(1)} all-gather(bf16[32,768]{1,0:T(8,128)(2,1)S(1)} %copy-done.2), channel_id=1, replica_groups=mesh['depth'=16,'row'=8,'col'=4] {'col'}, dimensions={0}, use_global_device_ids=true | all-gather | bytes 245760 | tf_op jit(solution)/shard_map/all_gather | solution.py:154
  32.0 0.0 copy-done
  32.0 3.1 %collective-permute-start = (bf16[384,768]{1,0:T(8,128)(2,1)S(1)}, bf16[384,768]{1,0:T(8,128)(2,1)S(1)}, u32[]{:S(2)}, u32[]{:S(2)}) collective-permute-start(bf16[384,768]{1,0:T(8,128)(2,1)S(1)} %bitcast.25), channel_id=1, source_target_pairs={{0,256},{32,288},{64,320},{96,352},{128,384},{160,416},{192,448},{... | collective-permute-start | bytes 1769480 | tf_op jit(solution)/shard_map/ppermute | solution.py:131
  35.1 11.9 %all_gather.7 = bf16[512,768]{1,0:T(8,128)(2,1)S(1)} all-gather(bf16[128,768]{1,0:T(8,128)(2,1)S(1)} %all_gather.6), channel_id=1, replica_groups={{0,64,128,192},{32,96,160,224},{256,320,384,448},{288,352,416,480},{1,6..., dimensions={0}, use_global_device_ids=true | all-gather | bytes 983040 | tf_op jit(solution)/shard_map/all_gather | solution.py:157
  47.0 0.0 collective-permute-done.refs_4_
  47.0 0.0 all-to-all-done
  47.0 7.7 %collective-permute-start.1 = (bf16[512,768]{1,0:T(8,128)(2,1)S(1)}, bf16[512,768]{1,0:T(8,128)(2,1)S(1)}, u32[]{:S(2)}, u32[]{:S(2)}) collective-permute-start(bf16[512,768]{1,0:T(8,128)(2,1)S(1)} %all_gather.7), channel_id=1, source_target_pairs={{0,32},{32,0},{64,96},{96,64},{128,160},{160,128},{192,224},{224,1... | collective-permute-start | bytes 2359304 | tf_op jit(solution)/shard_map/ppermute | solution.py:127
  54.8 1.9 %collective-permute-done.1 = bf16[512,768]{1,0:T(8,128)(2,1)S(1)} collective-permute-done((bf16[512,768]{1,0:T(8,128)(2,1)S(1)}, bf16[512,768]{1,0:T(8,128)(2,1)S(1)}, u32[]{:S(2)}, u32[]{:S(2)}) %collective-permute-start.1) | collective-permute-done | bytes 786464 | tf_op jit(solution)/shard_map/ppermute | solution.py:127
  56.7 1.5 %shard_map.52 = bf16[4,2,4,16,768]{4,3,2,1,0:T(8,128)(2,1)S(1)} custom-call(s32[3]{0:T(128)S(1)} %pad_add_fusion.s_ref.refs_0_, bf16[4,4,2,16,768]{4,3,2,1,0:T(8,128)(2,1)S(1)} %bitcast.13, bf16[4,4,2,16,768]{4,3,2,1,0:T(8,128)(2,1)S(1)} %bitcast.17, bf16[384,768]{1,0:T(8,128)(2,1)S(1)} %bitcast.26, bf16[384,768]{1,0:T(8,128)(2,1)S(1)} %collective-permute-done.refs_4_), custom_call_target="tpu_custom_call" | custom-call | tf_op jit(solution)/shard_map/pallas_call | solution.py:41
  58.2 4.4 %collective-permute-start.2 = (bf16[32,16,768]{2,1,0:T(8,128)(2,1)S(1)}, bf16[32,16,768]{2,1,0:T(8,128)(2,1)S(1)}, u32[]{:S(2)}, u32[]{:S(2)}) collective-permute-start(bf16[32,16,768]{2,1,0:T(8,128)(2,1)S(1)} %bitcast.28), channel_id=1, source_target_pairs={{0,4},{4,0},{8,12},{12,8},{16,20},{20,16},{24,28},{28,24},{32,60},... | collective-permute-start | bytes 2359304 | tf_op jit(solution)/shard_map/ppermute | solution.py:140
  62.6 2.1 %collective-permute-start.3 = (bf16[32,16,768]{2,1,0:T(8,128)(2,1)S(1)}, bf16[32,16,768]{2,1,0:T(8,128)(2,1)}, u32[]{:S(2)}, u32[]{:S(2)}) collective-permute-start(bf16[32,16,768]{2,1,0:T(8,128)(2,1)S(1)} %all-to-all-done), channel_id=1, source_target_pairs={{0,4},{4,0},{8,12},{12,8},{16,20},{20,16},{24,28},{28,24},{32,60},... | collective-permute-start | bytes 2359304 | tf_op jit(solution)/shard_map/ppermute | solution.py:140
  64.7 1.5 %shard_map.51 = bf16[4,2,4,16,768]{4,3,2,1,0:T(8,128)(2,1)S(1)} custom-call(s32[3]{0:T(128)S(1)} %pad_add_fusion.s_ref.refs_0_, bf16[4,4,2,16,768]{4,3,2,1,0:T(8,128)(2,1)S(1)} %bitcast.14, bf16[4,4,2,16,768]{4,3,2,1,0:T(8,128)(2,1)S(1)} %bitcast.18, bf16[384,768]{1,0:T(8,128)(2,1)S(1)} %bitcast.27, bf16[384,768]{1,0:T(8,128)(2,1)S(1)} %collective-permute-done.refs_4_), custom_call_target="tpu_custom_call" | custom-call | tf_op jit(solution)/shard_map/pallas_call | solution.py:41
  66.2 5.9 %collective-permute-done.2.b_ref = bf16[32,16,768]{2,1,0:T(8,128)(2,1)S(1)} collective-permute-done((bf16[32,16,768]{2,1,0:T(8,128)(2,1)S(1)}, bf16[32,16,768]{2,1,0:T(8,128)(2,1)S(1)}, u32[]{:S(2)}, u32[]{:S(2)}) %collective-permute-start.2) | collective-permute-done | bytes 786464 | tf_op jit(solution)/shard_map/ppermute | solution.py:140
  72.1 1.5 %shard_map.53 = bf16[32,16,768]{2,1,0:T(8,128)(2,1)} custom-call(s32[3]{0:T(128)S(1)} %pad_add_fusion.s_ref.refs_0_, bf16[32,16,768]{2,1,0:T(8,128)(2,1)S(1)} %bitcast.24, bf16[32,16,768]{2,1,0:T(8,128)(2,1)S(1)} %collective-permute-done.2.b_ref), custom_call_target="tpu_custom_call" | custom-call | tf_op jit(solution)/shard_map/pallas_call | solution.py:41
  73.6 8.1 %all-to-all-start.1 = ((bf16[32,16,768]{2,1,0:T(8,128)(2,1)}), bf16[32,16,768]{2,1,0:T(8,128)(2,1)S(1)}, u32[]{:S(2)}, u32[]{:S(2)}) async-start(bf16[32,16,768]{2,1,0:T(8,128)(2,1)} %shard_map.53), calls=%async_computation.1 | async-start | bytes 1572864 | tf_op jit(solution)/shard_map/all_to_all | solution.py:34
  81.7 0.0 collective-permute-done.3
  81.7 2.0 %shard_map.56 = bf16[384,768]{1,0:T(8,128)(2,1)S(1)} custom-call(s32[3]{0:T(128)S(1)} %pad_add_fusion.s_ref.refs_0_, bf16[4,2,4,16,768]{4,3,2,1,0:T(8,128)(2,1)S(1)} %bitcast.21, bf16[4,2,4,16,768]{4,3,2,1,0:T(8,128)(2,1)} %bitcast.11.refs_2_, bf16[4,4,2,16,768]{4,3,2,1,0:T(8,128)(2,1)S(1)} %bitcast.15, bf16[4,4,2,16,768]{4,3,2,1,0:T(8,128)(2,1)S(1)} %bitcast.19), custom_call_target="tpu_custom_call" | custom-call | flops 10000000000 | tf_op jit(solution)/shard_map/pallas_call | solution.py:41
  83.7 1.9 %collective-permute-start.4 = (bf16[384,768]{1,0:T(8,128)(2,1)S(1)}, bf16[384,768]{1,0:T(8,128)(2,1)S(1)}, u32[]{:S(2)}, u32[]{:S(2)}) collective-permute-start(bf16[384,768]{1,0:T(8,128)(2,1)S(1)} %shard_map.56), channel_id=1, source_target_pairs={{0,256},{32,288},{64,320},{96,352},{128,384},{160,416},{192,448},{... | collective-permute-start | bytes 1769480 | tf_op jit(solution)/shard_map/ppermute | solution.py:131
  85.7 2.0 %shard_map.55.a_ref = f32[384,768]{1,0:T(8,128)S(1)} custom-call(s32[3]{0:T(128)S(1)} %pad_add_fusion.s_ref.refs_0_, bf16[4,2,4,16,768]{4,3,2,1,0:T(8,128)(2,1)S(1)} %bitcast.22, bf16[4,2,4,16,768]{4,3,2,1,0:T(8,128)(2,1)} %bitcast.11.refs_2_, bf16[4,4,2,16,768]{4,3,2,1,0:T(8,128)(2,1)S(1)} %bitcast.16, bf16[4,4,2,16,768]{4,3,2,1,0:T(8,128)(2,1)S(1)} %bitcast.20), custom_call_target="tpu_custom_call" | custom-call | tf_op jit(solution)/shard_map/pallas_call | solution.py:41
  87.6 12.7 %collective-permute-done.4.b_ref = bf16[384,768]{1,0:T(8,128)(2,1)S(1)} collective-permute-done((bf16[384,768]{1,0:T(8,128)(2,1)S(1)}, bf16[384,768]{1,0:T(8,128)(2,1)S(1)}, u32[]{:S(2)}, u32[]{:S(2)}) %collective-permute-start.4) | collective-permute-done | bytes 589856 | tf_op jit(solution)/shard_map/ppermute | solution.py:131
  100.3 1.5 %shard_map.57 = bf16[384,768]{1,0:T(8,128)(2,1)} custom-call(s32[3]{0:T(128)S(1)} %pad_add_fusion.s_ref.refs_0_, f32[384,768]{1,0:T(8,128)S(1)} %shard_map.55.a_ref, bf16[384,768]{1,0:T(8,128)(2,1)S(1)} %collective-permute-done.4.b_ref), custom_call_target="tpu_custom_call" | custom-call | tf_op jit(solution)/shard_map/pallas_call | solution.py:41
  101.8 2.9 %all-to-all-done.1 = bf16[32,16,768]{2,1,0:T(8,128)(2,1)S(1)} async-done(((bf16[32,16,768]{2,1,0:T(8,128)(2,1)}), bf16[32,16,768]{2,1,0:T(8,128)(2,1)S(1)}, u32[]{:S(2)}, u32[]{:S(2)}) %all-to-all-start.1) | async-done | bytes 786464 | tf_op jit(solution)/shard_map/all_to_all | solution.py:34
  104.6 1.3 %shard_map.54 = bf16[16,6144]{1,0:T(8,128)(2,1)} custom-call(s32[3]{0:T(128)S(1)} %pad_add_fusion.s_ref.refs_0_, bf16[4,2,4,16,768]{4,3,2,1,0:T(8,128)(2,1)S(1)} %bitcast.23), custom_call_target="tpu_custom_call" | custom-call | tf_op jit(solution)/shard_map/pallas_call | solution.py:41
Async XLA Ops:
  0.7 0.9 copy-start.1
  1.7 12.7 %copy-start.2 = (bf16[32,768]{1,0:T(8,128)(2,1)S(1)}, bf16[32,768]{1,0:T(8,128)(2,1)}, u32[]{:S(2)}) copy-start(bf16[32,768]{1,0:T(8,128)(2,1)} %param.4) | copy-start | bytes 147460
  1.7 30.4 %copy-start = (bf16[1,384,768]{2,1,0:T(8,128)(2,1)S(1)}, bf16[1,384,768]{2,1,0:T(8,128)(2,1)}, u32[]{:S(2)}) copy-start(bf16[1,384,768]{2,1,0:T(8,128)(2,1)} %param.5) | copy-start | bytes 1769476
  3.2 43.9 %all-to-all-start = ((bf16[32,16,768]{2,1,0:T(8,128)(2,1)}), bf16[32,16,768]{2,1,0:T(8,128)(2,1)S(1)}, u32[]{:S(2)}, u32[]{:S(2)}) async-start(bf16[32,16,768]{2,1,0:T(8,128)(2,1)} %bitcast.3), calls=%async_computation | async-start | bytes 1572864 | tf_op jit(solution)/shard_map/all_to_all | solution.py:34
  32.0 15.0 %collective-permute-start = (bf16[384,768]{1,0:T(8,128)(2,1)S(1)}, bf16[384,768]{1,0:T(8,128)(2,1)S(1)}, u32[]{:S(2)}, u32[]{:S(2)}) collective-permute-start(bf16[384,768]{1,0:T(8,128)(2,1)S(1)} %bitcast.25), channel_id=1, source_target_pairs={{0,256},{32,288},{64,320},{96,352},{128,384},{160,416},{192,448},{... | collective-permute-start | bytes 1769480 | tf_op jit(solution)/shard_map/ppermute | solution.py:131
  47.0 9.6 %collective-permute-start.1 = (bf16[512,768]{1,0:T(8,128)(2,1)S(1)}, bf16[512,768]{1,0:T(8,128)(2,1)S(1)}, u32[]{:S(2)}, u32[]{:S(2)}) collective-permute-start(bf16[512,768]{1,0:T(8,128)(2,1)S(1)} %all_gather.7), channel_id=1, source_target_pairs={{0,32},{32,0},{64,96},{96,64},{128,160},{160,128},{192,224},{224,1... | collective-permute-start | bytes 2359304 | tf_op jit(solution)/shard_map/ppermute | solution.py:127
  58.2 13.9 %collective-permute-start.2 = (bf16[32,16,768]{2,1,0:T(8,128)(2,1)S(1)}, bf16[32,16,768]{2,1,0:T(8,128)(2,1)S(1)}, u32[]{:S(2)}, u32[]{:S(2)}) collective-permute-start(bf16[32,16,768]{2,1,0:T(8,128)(2,1)S(1)} %bitcast.28), channel_id=1, source_target_pairs={{0,4},{4,0},{8,12},{12,8},{16,20},{20,16},{24,28},{28,24},{32,60},... | collective-permute-start | bytes 2359304 | tf_op jit(solution)/shard_map/ppermute | solution.py:140
  62.6 19.2 %collective-permute-start.3 = (bf16[32,16,768]{2,1,0:T(8,128)(2,1)S(1)}, bf16[32,16,768]{2,1,0:T(8,128)(2,1)}, u32[]{:S(2)}, u32[]{:S(2)}) collective-permute-start(bf16[32,16,768]{2,1,0:T(8,128)(2,1)S(1)} %all-to-all-done), channel_id=1, source_target_pairs={{0,4},{4,0},{8,12},{12,8},{16,20},{20,16},{24,28},{28,24},{32,60},... | collective-permute-start | bytes 2359304 | tf_op jit(solution)/shard_map/ppermute | solution.py:140
  73.6 31.0 %all-to-all-start.1 = ((bf16[32,16,768]{2,1,0:T(8,128)(2,1)}), bf16[32,16,768]{2,1,0:T(8,128)(2,1)S(1)}, u32[]{:S(2)}, u32[]{:S(2)}) async-start(bf16[32,16,768]{2,1,0:T(8,128)(2,1)} %shard_map.53), calls=%async_computation.1 | async-start | bytes 1572864 | tf_op jit(solution)/shard_map/all_to_all | solution.py:34
  83.7 16.6 %collective-permute-start.4 = (bf16[384,768]{1,0:T(8,128)(2,1)S(1)}, bf16[384,768]{1,0:T(8,128)(2,1)S(1)}, u32[]{:S(2)}, u32[]{:S(2)}) collective-permute-start(bf16[384,768]{1,0:T(8,128)(2,1)S(1)} %shard_map.56), channel_id=1, source_target_pairs={{0,256},{32,288},{64,320},{96,352},{128,384},{160,416},{192,448},{... | collective-permute-start | bytes 1769480 | tf_op jit(solution)/shard_map/ppermute | solution.py:131

commit v4 on v3

--- a/solution.py
+++ b/solution.py
@@ -49,13 +49,17 @@
     )(scalars, *operands)
 
 
-def spread_kernel(s_ref, x_ref, o_ref):
-    for x in range(NX):
-        for core in range(2):
-            for zl in range(NZ):
-                block = x_ref[:, pl.ds(depth_of(zl, x, core) * B, B)]
-                for y4 in range(NY // 2):
-                    o_ref[x, core, y4, :, pl.ds(zl * B, B)] = block
+def spread_rows(x):
+    blocks = [
+        jnp.concatenate(
+            [x[:, depth_of(zl, i, core) * B : (depth_of(zl, i, core) + 1) * B] for zl in range(NZ)],
+            axis=1,
+        )
+        for i in range(NX)
+        for core in range(2)
+    ]
+    one = jnp.stack(blocks).reshape(NX, 2, 1, T, 2 * B)
+    return jnp.broadcast_to(one, (NX, 2, NY // 2, T, 2 * B))
 
 
 def block_at(zl):
@@ -102,11 +106,6 @@
     o_ref[...] = weight_product(s_ref, mine_ref, theirs_ref, g_ref, h_ref, flip).astype(o_ref.dtype)
 
 
-def add_kernel(s_ref, a_ref, b_ref, o_ref):
-    for i in range(NX * NY):
-        o_ref[i] = a_ref[i] + b_ref[i]
-
-
 def last_kernel(s_ref, a_ref, b_ref, o_ref):
     o_ref[...] = (a_ref[...] + b_ref[...].astype(jnp.float32)).astype(o_ref.dtype)
 
@@ -149,7 +148,7 @@
     half = shape((NX, 2, NY // 2, T, 2 * B), bf)
     flat = (NX * NY, T, 2 * B)
 
-    spread = call(spread_kernel, half, s, inputs)
+    spread = spread_rows(inputs)
     mine = exchange(spread.reshape(flat), ("depth", "row"), token_groups())
     slab = lax.all_gather(grad_out, "col", axis=0, tiled=True)
     slab, w = lax.optimization_barrier((slab, w))
@@ -182,7 +181,7 @@
             cost=cost,
         )
 
-    part = call(add_kernel, shape(flat, bf), s, terms(False), got)
+    part = terms(False) + got
     summed = exchange(part, ("depth", "row"), token_groups())
     grad_inputs = call(sum_kernel, shape((T, 16 * B), bf), s, summed.reshape(half.shape))
     crossed = swap_z(weight_term(True, bf, 10**10))

time: 107 us -> 106 us (level)
  Pallas kernels: 12.8 us -> 9.76 us
  other arithmetic: 0.08 us -> 1.18 us
    pallas_call x8 -> x6, Pallas kernels: 12.8 us -> 9.76 us  [call(): pl.pallas_call(kernel, out_shape=out_shape, in_specs=[pl.BlockSpec(memory...]
  transfers between devices with their start and end apart: 7 -> 7, of which waited for: 4 -> 4; matrix products, arithmetic and copies ran while one was open for 0% -> 1% of each run, Pallas kernels for 8% -> 7%
where the time goes in v4:
time: 106 us; the launch traced here: 105 us
  starting transfers between devices  38.5 us (36%)
  blocking collectives  29.5 us (28%)
  waiting for transfers between devices  23.3 us (22%)
  Pallas kernels  9.76 us (9%)
  local copies, waits for them, and re-layouts  1.87 us (2%)
  other arithmetic  1.18 us (1%)
    all_to_all x2, starting transfers between devices, exchange(): lax.all_to_all(x, axes, split_axis=0, concat_axis=0, axis_index_groups=gr...  19.3 us
    all_gather x1, blocking collectives, local(): slab = lax.all_gather(grad_out, 'col', axis=0, tiled=True)  17.6 us
    ppermute x2, waiting for transfers between devices, swap_z(): return lax.ppermute(x, 'depth', [(i, i ^ 8) for i in range(16)])  12.7 us
    all_gather x1, blocking collectives, local(): lax.all_gather(slab, 'depth', axis=0, tiled=True, axis_index_groups=x_gro...  11.9 us
    pallas_call x6, Pallas kernels, call(): pl.pallas_call(kernel, out_shape=out_shape, in_specs=[pl.BlockSpec(memory...  9.76 us
    ppermute x1, starting transfers between devices, swap_core(): return lax.ppermute(x, 'depth', [(i, i ^ 1) for i in range(16)])  7.74 us
    ppermute x2, starting transfers between devices, swap_row(): return lax.ppermute(x, ('depth', 'row'), pairs)  6.49 us
    ppermute x2, waiting for transfers between devices, swap_row(): return lax.ppermute(x, ('depth', 'row'), pairs)  5.91 us
  transfers between devices with their start and end apart: 7, of which 4 were waited for; matrix products, arithmetic and copies ran while one was open for 1% of the time, Pallas kernels for 7%

profile of v4, /device:TPU:1, one launch (start us, length us, event | category | flops | bytes accessed | tf_op | source)
XLA Modules:
  0.0 105.0 jit_solution(3476091752043088908)
XLA Ops:
  0.6 0.9 fusion.8
  1.6 0.0 copy-start.1
  1.7 0.0 copy-start
  1.7 0.9 broadcast_in_dim.8
  2.6 11.2 %all-to-all-start = ((bf16[32,16,768]{2,1,0:T(8,128)(2,1)}), bf16[32,16,768]{2,1,0:T(8,128)(2,1)S(1)}, u32[]{:S(2)}, u32[]{:S(2)}) async-start(bf16[32,16,768]{2,1,0:T(8,128)(2,1)} %bitcast.12), calls=%async_computation | async-start | bytes 1572864 | tf_op jit(solution)/shard_map/all_to_all | solution.py:34
  13.8 0.0 copy-done.1
  13.9 17.6 %all_gather.6 = bf16[128,768]{1,0:T(8,128)(2,1)S(1)} all-gather(bf16[32,768]{1,0:T(8,128)(2,1)S(1)} %copy-done.1), channel_id=1, replica_groups=mesh['depth'=16,'row'=8,'col'=4] {'col'}, dimensions={0}, use_global_device_ids=true | all-gather | bytes 245760 | tf_op jit(solution)/shard_map/all_gather | solution.py:153
  31.5 0.0 copy-done
  31.5 3.1 %collective-permute-start = (bf16[384,768]{1,0:T(8,128)(2,1)S(1)}, bf16[384,768]{1,0:T(8,128)(2,1)S(1)}, u32[]{:S(2)}, u32[]{:S(2)}) collective-permute-start(bf16[384,768]{1,0:T(8,128)(2,1)S(1)} %bitcast.58), channel_id=1, source_target_pairs={{0,256},{32,288},{64,320},{96,352},{128,384},{160,416},{192,448},{... | collective-permute-start | bytes 1769480 | tf_op jit(solution)/shard_map/ppermute | solution.py:130
  34.6 11.9 %all_gather.7 = bf16[512,768]{1,0:T(8,128)(2,1)S(1)} all-gather(bf16[128,768]{1,0:T(8,128)(2,1)S(1)} %all_gather.6), channel_id=1, replica_groups={{0,64,128,192},{32,96,160,224},{256,320,384,448},{288,352,416,480},{1,6..., dimensions={0}, use_global_device_ids=true | all-gather | bytes 983040 | tf_op jit(solution)/shard_map/all_gather | solution.py:156
  46.5 0.0 collective-permute-done.refs_4_
  46.5 0.0 all-to-all-done
  46.5 7.7 %collective-permute-start.1 = (bf16[512,768]{1,0:T(8,128)(2,1)S(1)}, bf16[512,768]{1,0:T(8,128)(2,1)S(1)}, u32[]{:S(2)}, u32[]{:S(2)}) collective-permute-start(bf16[512,768]{1,0:T(8,128)(2,1)S(1)} %all_gather.7), channel_id=1, source_target_pairs={{0,32},{32,0},{64,96},{96,64},{128,160},{160,128},{192,224},{224,1... | collective-permute-start | bytes 2359304 | tf_op jit(solution)/shard_map/ppermute | solution.py:126
  54.3 0.1 pad_add_fusion.refs_0_.s_ref
  54.3 1.8 %collective-permute-done.1 = bf16[512,768]{1,0:T(8,128)(2,1)S(1)} collective-permute-done((bf16[512,768]{1,0:T(8,128)(2,1)S(1)}, bf16[512,768]{1,0:T(8,128)(2,1)S(1)}, u32[]{:S(2)}, u32[]{:S(2)}) %collective-permute-start.1) | collective-permute-done | bytes 786464 | tf_op jit(solution)/shard_map/ppermute | solution.py:126
  56.1 1.5 %shard_map.51 = bf16[4,2,4,16,768]{4,3,2,1,0:T(8,128)(2,1)S(1)} custom-call(s32[3]{0:T(128)S(1)} %pad_add_fusion.refs_0_.s_ref, bf16[4,4,2,16,768]{4,3,2,1,0:T(8,128)(2,1)S(1)} %bitcast.47, bf16[4,4,2,16,768]{4,3,2,1,0:T(8,128)(2,1)S(1)} %bitcast.51, bf16[384,768]{1,0:T(8,128)(2,1)S(1)} %bitcast.59, bf16[384,768]{1,0:T(8,128)(2,1)S(1)} %collective-permute-done.refs_4_), custom_call_target="tpu_custom_call" | custom-call | tf_op jit(solution)/shard_map/pallas_call | solution.py:41
  57.6 4.4 %collective-permute-start.2 = (bf16[32,16,768]{2,1,0:T(8,128)(2,1)S(1)}, bf16[32,16,768]{2,1,0:T(8,128)(2,1)S(1)}, u32[]{:S(2)}, u32[]{:S(2)}) collective-permute-start(bf16[32,16,768]{2,1,0:T(8,128)(2,1)S(1)} %bitcast.61), channel_id=1, source_target_pairs={{0,4},{4,0},{8,12},{12,8},{16,20},{20,16},{24,28},{28,24},{32,60},... | collective-permute-start | bytes 2359304 | tf_op jit(solution)/shard_map/ppermute | solution.py:139
  62.0 2.1 %collective-permute-start.3 = (bf16[32,16,768]{2,1,0:T(8,128)(2,1)S(1)}, bf16[32,16,768]{2,1,0:T(8,128)(2,1)}, u32[]{:S(2)}, u32[]{:S(2)}) collective-permute-start(bf16[32,16,768]{2,1,0:T(8,128)(2,1)S(1)} %all-to-all-done), channel_id=1, source_target_pairs={{0,4},{4,0},{8,12},{12,8},{16,20},{20,16},{24,28},{28,24},{32,60},... | collective-permute-start | bytes 2359304 | tf_op jit(solution)/shard_map/ppermute | solution.py:139
  64.1 1.5 %shard_map.50 = bf16[4,2,4,16,768]{4,3,2,1,0:T(8,128)(2,1)S(1)} custom-call(s32[3]{0:T(128)S(1)} %pad_add_fusion.refs_0_.s_ref, bf16[4,4,2,16,768]{4,3,2,1,0:T(8,128)(2,1)S(1)} %bitcast.48, bf16[4,4,2,16,768]{4,3,2,1,0:T(8,128)(2,1)S(1)} %bitcast.52, bf16[384,768]{1,0:T(8,128)(2,1)S(1)} %bitcast.60, bf16[384,768]{1,0:T(8,128)(2,1)S(1)} %collective-permute-done.refs_4_), custom_call_target="tpu_custom_call" | custom-call | tf_op jit(solution)/shard_map/pallas_call | solution.py:41
  65.7 5.9 %collective-permute-done.2 = bf16[32,16,768]{2,1,0:T(8,128)(2,1)S(1)} collective-permute-done((bf16[32,16,768]{2,1,0:T(8,128)(2,1)S(1)}, bf16[32,16,768]{2,1,0:T(8,128)(2,1)S(1)}, u32[]{:S(2)}, u32[]{:S(2)}) %collective-permute-start.2) | collective-permute-done | bytes 786464 | tf_op jit(solution)/shard_map/ppermute | solution.py:139
  71.6 1.1 %bitcast_add_fusion = bf16[32,16,768]{2,1,0:T(8,128)(2,1)} fusion(bf16[32,16,768]{2,1,0:T(8,128)(2,1)S(1)} %collective-permute-done.2, bf16[4,2,4,16,768]{4,3,2,1,0:T(8,128)(2,1)S(1)} %shard_map.50), kind=kLoop, calls=%fused_computation | loop fusion | flops 393216 | bytes 2359296 | tf_op jit(solution)/shard_map/add | solution.py:184
  72.6 8.1 %all-to-all-start.1 = ((bf16[32,16,768]{2,1,0:T(8,128)(2,1)}), bf16[32,16,768]{2,1,0:T(8,128)(2,1)S(1)}, u32[]{:S(2)}, u32[]{:S(2)}) async-start(bf16[32,16,768]{2,1,0:T(8,128)(2,1)} %bitcast_add_fusion), calls=%async_computation.1 | async-start | bytes 1572864 | tf_op jit(solution)/shard_map/all_to_all | solution.py:34
  80.7 0.0 collective-permute-done.3
  80.7 2.0 %shard_map.54 = bf16[384,768]{1,0:T(8,128)(2,1)S(1)} custom-call(s32[3]{0:T(128)S(1)} %pad_add_fusion.refs_0_.s_ref, bf16[4,2,4,16,768]{4,3,2,1,0:T(8,128)(2,1)S(1)} %bitcast.55, bf16[4,2,4,16,768]{4,3,2,1,0:T(8,128)(2,1)} %bitcast.20.refs_2_, bf16[4,4,2,16,768]{4,3,2,1,0:T(8,128)(2,1)S(1)} %bitcast.49, bf16[4,4,2,16,768]{4,3,2,1,0:T(8,128)(2,1)S(1)} %bitcast.53), custom_call_target="tpu_custom_call" | custom-call | flops 10000000000 | tf_op jit(solution)/shard_map/pallas_call | solution.py:41
  82.7 1.9 %collective-permute-start.4 = (bf16[384,768]{1,0:T(8,128)(2,1)S(1)}, bf16[384,768]{1,0:T(8,128)(2,1)S(1)}, u32[]{:S(2)}, u32[]{:S(2)}) collective-permute-start(bf16[384,768]{1,0:T(8,128)(2,1)S(1)} %shard_map.54), channel_id=1, source_target_pairs={{0,256},{32,288},{64,320},{96,352},{128,384},{160,416},{192,448},{... | collective-permute-start | bytes 1769480 | tf_op jit(solution)/shard_map/ppermute | solution.py:130
  84.7 2.0 %shard_map.53.a_ref = f32[384,768]{1,0:T(8,128)S(1)} custom-call(s32[3]{0:T(128)S(1)} %pad_add_fusion.refs_0_.s_ref, bf16[4,2,4,16,768]{4,3,2,1,0:T(8,128)(2,1)S(1)} %bitcast.56, bf16[4,2,4,16,768]{4,3,2,1,0:T(8,128)(2,1)} %bitcast.20.refs_2_, bf16[4,4,2,16,768]{4,3,2,1,0:T(8,128)(2,1)S(1)} %bitcast.50, bf16[4,4,2,16,768]{4,3,2,1,0:T(8,128)(2,1)S(1)} %bitcast.54), custom_call_target="tpu_custom_call" | custom-call | tf_op jit(solution)/shard_map/pallas_call | solution.py:41
  86.6 12.7 %collective-permute-done.4.b_ref = bf16[384,768]{1,0:T(8,128)(2,1)S(1)} collective-permute-done((bf16[384,768]{1,0:T(8,128)(2,1)S(1)}, bf16[384,768]{1,0:T(8,128)(2,1)S(1)}, u32[]{:S(2)}, u32[]{:S(2)}) %collective-permute-start.4) | collective-permute-done | bytes 589856 | tf_op jit(solution)/shard_map/ppermute | solution.py:130
  99.3 1.5 %shard_map.55 = bf16[384,768]{1,0:T(8,128)(2,1)} custom-call(s32[3]{0:T(128)S(1)} %pad_add_fusion.refs_0_.s_ref, f32[384,768]{1,0:T(8,128)S(1)} %shard_map.53.a_ref, bf16[384,768]{1,0:T(8,128)(2,1)S(1)} %collective-permute-done.4.b_ref), custom_call_target="tpu_custom_call" | custom-call | tf_op jit(solution)/shard_map/pallas_call | solution.py:41
  100.8 2.9 %all-to-all-done.1 = bf16[32,16,768]{2,1,0:T(8,128)(2,1)S(1)} async-done(((bf16[32,16,768]{2,1,0:T(8,128)(2,1)}), bf16[32,16,768]{2,1,0:T(8,128)(2,1)S(1)}, u32[]{:S(2)}, u32[]{:S(2)}) %all-to-all-start.1) | async-done | bytes 786464 | tf_op jit(solution)/shard_map/all_to_all | solution.py:34
  103.6 1.3 %shard_map.52 = bf16[16,6144]{1,0:T(8,128)(2,1)} custom-call(s32[3]{0:T(128)S(1)} %pad_add_fusion.refs_0_.s_ref, bf16[4,2,4,16,768]{4,3,2,1,0:T(8,128)(2,1)S(1)} %bitcast.57), custom_call_target="tpu_custom_call" | custom-call | tf_op jit(solution)/shard_map/pallas_call | solution.py:41
  (8 shorter events, 0.0 us)
Async XLA Ops:
  1.6 12.2 %copy-start.1 = (bf16[32,768]{1,0:T(8,128)(2,1)S(1)}, bf16[32,768]{1,0:T(8,128)(2,1)}, u32[]{:S(2)}) copy-start(bf16[32,768]{1,0:T(8,128)(2,1)} %param.4) | copy-start | bytes 147460
  1.7 29.8 %copy-start = (bf16[1,384,768]{2,1,0:T(8,128)(2,1)S(1)}, bf16[1,384,768]{2,1,0:T(8,128)(2,1)}, u32[]{:S(2)}) copy-start(bf16[1,384,768]{2,1,0:T(8,128)(2,1)} %param.5) | copy-start | bytes 1769476
  2.6 43.9 %all-to-all-start = ((bf16[32,16,768]{2,1,0:T(8,128)(2,1)}), bf16[32,16,768]{2,1,0:T(8,128)(2,1)S(1)}, u32[]{:S(2)}, u32[]{:S(2)}) async-start(bf16[32,16,768]{2,1,0:T(8,128)(2,1)} %bitcast.12), calls=%async_computation | async-start | bytes 1572864 | tf_op jit(solution)/shard_map/all_to_all | solution.py:34
  31.5 15.0 %collective-permute-start = (bf16[384,768]{1,0:T(8,128)(2,1)S(1)}, bf16[384,768]{1,0:T(8,128)(2,1)S(1)}, u32[]{:S(2)}, u32[]{:S(2)}) collective-permute-start(bf16[384,768]{1,0:T(8,128)(2,1)S(1)} %bitcast.58), channel_id=1, source_target_pairs={{0,256},{32,288},{64,320},{96,352},{128,384},{160,416},{192,448},{... | collective-permute-start | bytes 1769480 | tf_op jit(solution)/shard_map/ppermute | solution.py:130
  46.5 9.6 %collective-permute-start.1 = (bf16[512,768]{1,0:T(8,128)(2,1)S(1)}, bf16[512,768]{1,0:T(8,128)(2,1)S(1)}, u32[]{:S(2)}, u32[]{:S(2)}) collective-permute-start(bf16[512,768]{1,0:T(8,128)(2,1)S(1)} %all_gather.7), channel_id=1, source_target_pairs={{0,32},{32,0},{64,96},{96,64},{128,160},{160,128},{192,224},{224,1... | collective-permute-start | bytes 2359304 | tf_op jit(solution)/shard_map/ppermute | solution.py:126
  57.6 13.9 %collective-permute-start.2 = (bf16[32,16,768]{2,1,0:T(8,128)(2,1)S(1)}, bf16[32,16,768]{2,1,0:T(8,128)(2,1)S(1)}, u32[]{:S(2)}, u32[]{:S(2)}) collective-permute-start(bf16[32,16,768]{2,1,0:T(8,128)(2,1)S(1)} %bitcast.61), channel_id=1, source_target_pairs={{0,4},{4,0},{8,12},{12,8},{16,20},{20,16},{24,28},{28,24},{32,60},... | collective-permute-start | bytes 2359304 | tf_op jit(solution)/shard_map/ppermute | solution.py:139
  62.0 18.7 %collective-permute-start.3 = (bf16[32,16,768]{2,1,0:T(8,128)(2,1)S(1)}, bf16[32,16,768]{2,1,0:T(8,128)(2,1)}, u32[]{:S(2)}, u32[]{:S(2)}) collective-permute-start(bf16[32,16,768]{2,1,0:T(8,128)(2,1)S(1)} %all-to-all-done), channel_id=1, source_target_pairs={{0,4},{4,0},{8,12},{12,8},{16,20},{20,16},{24,28},{28,24},{32,60},... | collective-permute-start | bytes 2359304 | tf_op jit(solution)/shard_map/ppermute | solution.py:139
  72.6 31.0 %all-to-all-start.1 = ((bf16[32,16,768]{2,1,0:T(8,128)(2,1)}), bf16[32,16,768]{2,1,0:T(8,128)(2,1)S(1)}, u32[]{:S(2)}, u32[]{:S(2)}) async-start(bf16[32,16,768]{2,1,0:T(8,128)(2,1)} %bitcast_add_fusion), calls=%async_computation.1 | async-start | bytes 1572864 | tf_op jit(solution)/shard_map/all_to_all | solution.py:34
  82.7 16.6 %collective-permute-start.4 = (bf16[384,768]{1,0:T(8,128)(2,1)S(1)}, bf16[384,768]{1,0:T(8,128)(2,1)S(1)}, u32[]{:S(2)}, u32[]{:S(2)}) collective-permute-start(bf16[384,768]{1,0:T(8,128)(2,1)S(1)} %shard_map.54), channel_id=1, source_target_pairs={{0,256},{32,288},{64,320},{96,352},{128,384},{160,416},{192,448},{... | collective-permute-start | bytes 1769480 | tf_op jit(solution)/shard_map/ppermute | solution.py:130

commit v5 on v4

--- a/solution.py
+++ b/solution.py
@@ -73,14 +73,13 @@
 def terms_kernel(other, s_ref, g_ref, h_ref, w_ref, v_ref, o_ref):
     zl, core, parity = s_ref[0], s_ref[1], s_ref[2]
     at = 1 - parity if other else parity
-    g = jnp.concatenate([rows_at(g_ref, at), rows_at(h_ref, at)], axis=0)
-    for w, z in ((w_ref, zl), (v_ref, 1 - zl)):
-        total = lax.dot_general(
-            g, w[...], (((1,), (1,)), ((), ())), preferred_element_type=jnp.float32
-        ).astype(jnp.bfloat16)
-        total = total.reshape(2, NX, NY // 2, T, B)
-        o_ref[:, core, :, :, block_at(z)] = total[0]
-        o_ref[:, 1 - core, :, :, block_at(z)] = total[1]
+    for rows, c in ((g_ref, core), (h_ref, 1 - core)):
+        g = rows_at(rows, at)
+        for w, z in ((w_ref, zl), (v_ref, 1 - zl)):
+            total = lax.dot_general(
+                g, w[...], (((1,), (1,)), ((), ())), preferred_element_type=jnp.float32
+            ).astype(jnp.bfloat16)
+            o_ref[:, c, :, :, block_at(z)] = total.reshape(NX, NY // 2, T, B)
 
 
 def weight_product(s_ref, mine_ref, theirs_ref, g_ref, h_ref, flip_z):

time: 106 us -> 106 us (level)
  no operation moved by 1% of the time
where the time goes in v5:
time: 106 us; the launch traced here: 105 us
  starting transfers between devices  38.5 us (36%)
  blocking collectives  29.5 us (28%)
  waiting for transfers between devices  23.3 us (22%)
  Pallas kernels  9.77 us (9%)
  local copies, waits for them, and re-layouts  1.87 us (2%)
  other arithmetic  1.18 us (1%)
    all_to_all x2, starting transfers between devices, exchange(): lax.all_to_all(x, axes, split_axis=0, concat_axis=0, axis_index_groups=gr...  19.3 us
    all_gather x1, blocking collectives, local(): slab = lax.all_gather(grad_out, 'col', axis=0, tiled=True)  17.6 us
    ppermute x2, waiting for transfers between devices, swap_z(): return lax.ppermute(x, 'depth', [(i, i ^ 8) for i in range(16)])  12.7 us
    all_gather x1, blocking collectives, local(): lax.all_gather(slab, 'depth', axis=0, tiled=True, axis_index_groups=x_gro...  11.9 us
    pallas_call x6, Pallas kernels, call(): pl.pallas_call(kernel, out_shape=out_shape, in_specs=[pl.BlockSpec(memory...  9.77 us
    ppermute x1, starting transfers between devices, swap_core(): return lax.ppermute(x, 'depth', [(i, i ^ 1) for i in range(16)])  7.74 us
    ppermute x2, starting transfers between devices, swap_row(): return lax.ppermute(x, ('depth', 'row'), pairs)  6.49 us
    ppermute x2, waiting for transfers between devices, swap_row(): return lax.ppermute(x, ('depth', 'row'), pairs)  5.91 us
  transfers between devices with their start and end apart: 7, of which 4 were waited for; matrix products, arithmetic and copies ran while one was open for 1% of the time, Pallas kernels for 7%

profile of v5, /device:TPU:1, one launch (start us, length us, event | category | flops | bytes accessed | tf_op | source)
XLA Modules:
  0.0 105.0 jit_solution(17476406889358465133)
XLA Ops:
  0.6 0.9 fusion.8
  1.6 0.0 copy-start.1
  1.7 0.0 copy-start
  1.7 0.9 broadcast_in_dim.8
  2.6 11.2 %all-to-all-start = ((bf16[32,16,768]{2,1,0:T(8,128)(2,1)}), bf16[32,16,768]{2,1,0:T(8,128)(2,1)S(1)}, u32[]{:S(2)}, u32[]{:S(2)}) async-start(bf16[32,16,768]{2,1,0:T(8,128)(2,1)} %bitcast.12), calls=%async_computation | async-start | bytes 1572864 | tf_op jit(solution)/shard_map/all_to_all | solution.py:34
  13.8 0.0 copy-done.1
  13.9 17.6 %all_gather.6 = bf16[128,768]{1,0:T(8,128)(2,1)S(1)} all-gather(bf16[32,768]{1,0:T(8,128)(2,1)S(1)} %copy-done.1), channel_id=1, replica_groups=mesh['depth'=16,'row'=8,'col'=4] {'col'}, dimensions={0}, use_global_device_ids=true | all-gather | bytes 245760 | tf_op jit(solution)/shard_map/all_gather | solution.py:152
  31.5 0.0 copy-done
  31.5 3.1 %collective-permute-start = (bf16[384,768]{1,0:T(8,128)(2,1)S(1)}, bf16[384,768]{1,0:T(8,128)(2,1)S(1)}, u32[]{:S(2)}, u32[]{:S(2)}) collective-permute-start(bf16[384,768]{1,0:T(8,128)(2,1)S(1)} %bitcast.58), channel_id=1, source_target_pairs={{0,256},{32,288},{64,320},{96,352},{128,384},{160,416},{192,448},{... | collective-permute-start | bytes 1769480 | tf_op jit(solution)/shard_map/ppermute | solution.py:129
  34.6 11.9 %all_gather.7 = bf16[512,768]{1,0:T(8,128)(2,1)S(1)} all-gather(bf16[128,768]{1,0:T(8,128)(2,1)S(1)} %all_gather.6), channel_id=1, replica_groups={{0,64,128,192},{32,96,160,224},{256,320,384,448},{288,352,416,480},{1,6..., dimensions={0}, use_global_device_ids=true | all-gather | bytes 983040 | tf_op jit(solution)/shard_map/all_gather | solution.py:155
  46.5 0.0 collective-permute-done.refs_4_
  46.5 0.0 all-to-all-done
  46.5 7.7 %collective-permute-start.1 = (bf16[512,768]{1,0:T(8,128)(2,1)S(1)}, bf16[512,768]{1,0:T(8,128)(2,1)S(1)}, u32[]{:S(2)}, u32[]{:S(2)}) collective-permute-start(bf16[512,768]{1,0:T(8,128)(2,1)S(1)} %all_gather.7), channel_id=1, source_target_pairs={{0,32},{32,0},{64,96},{96,64},{128,160},{160,128},{192,224},{224,1... | collective-permute-start | bytes 2359304 | tf_op jit(solution)/shard_map/ppermute | solution.py:125
  54.3 0.1 pad_add_fusion.refs_0_.s_ref
  54.3 1.8 %collective-permute-done.1 = bf16[512,768]{1,0:T(8,128)(2,1)S(1)} collective-permute-done((bf16[512,768]{1,0:T(8,128)(2,1)S(1)}, bf16[512,768]{1,0:T(8,128)(2,1)S(1)}, u32[]{:S(2)}, u32[]{:S(2)}) %collective-permute-start.1) | collective-permute-done | bytes 786464 | tf_op jit(solution)/shard_map/ppermute | solution.py:125
  56.1 1.5 %shard_map.51 = bf16[4,2,4,16,768]{4,3,2,1,0:T(8,128)(2,1)S(1)} custom-call(s32[3]{0:T(128)S(1)} %pad_add_fusion.refs_0_.s_ref, bf16[4,4,2,16,768]{4,3,2,1,0:T(8,128)(2,1)S(1)} %bitcast.47, bf16[4,4,2,16,768]{4,3,2,1,0:T(8,128)(2,1)S(1)} %bitcast.51, bf16[384,768]{1,0:T(8,128)(2,1)S(1)} %bitcast.59, bf16[384,768]{1,0:T(8,128)(2,1)S(1)} %collective-permute-done.refs_4_), custom_call_target="tpu_custom_call" | custom-call | tf_op jit(solution)/shard_map/pallas_call | solution.py:41
  57.6 4.4 %collective-permute-start.2 = (bf16[32,16,768]{2,1,0:T(8,128)(2,1)S(1)}, bf16[32,16,768]{2,1,0:T(8,128)(2,1)S(1)}, u32[]{:S(2)}, u32[]{:S(2)}) collective-permute-start(bf16[32,16,768]{2,1,0:T(8,128)(2,1)S(1)} %bitcast.61), channel_id=1, source_target_pairs={{0,4},{4,0},{8,12},{12,8},{16,20},{20,16},{24,28},{28,24},{32,60},... | collective-permute-start | bytes 2359304 | tf_op jit(solution)/shard_map/ppermute | solution.py:138
  62.0 2.1 %collective-permute-start.3 = (bf16[32,16,768]{2,1,0:T(8,128)(2,1)S(1)}, bf16[32,16,768]{2,1,0:T(8,128)(2,1)}, u32[]{:S(2)}, u32[]{:S(2)}) collective-permute-start(bf16[32,16,768]{2,1,0:T(8,128)(2,1)S(1)} %all-to-all-done), channel_id=1, source_target_pairs={{0,4},{4,0},{8,12},{12,8},{16,20},{20,16},{24,28},{28,24},{32,60},... | collective-permute-start | bytes 2359304 | tf_op jit(solution)/shard_map/ppermute | solution.py:138
  64.2 1.5 %shard_map.50 = bf16[4,2,4,16,768]{4,3,2,1,0:T(8,128)(2,1)S(1)} custom-call(s32[3]{0:T(128)S(1)} %pad_add_fusion.refs_0_.s_ref, bf16[4,4,2,16,768]{4,3,2,1,0:T(8,128)(2,1)S(1)} %bitcast.48, bf16[4,4,2,16,768]{4,3,2,1,0:T(8,128)(2,1)S(1)} %bitcast.52, bf16[384,768]{1,0:T(8,128)(2,1)S(1)} %bitcast.60, bf16[384,768]{1,0:T(8,128)(2,1)S(1)} %collective-permute-done.refs_4_), custom_call_target="tpu_custom_call" | custom-call | tf_op jit(solution)/shard_map/pallas_call | solution.py:41
  65.7 5.9 %collective-permute-done.2 = bf16[32,16,768]{2,1,0:T(8,128)(2,1)S(1)} collective-permute-done((bf16[32,16,768]{2,1,0:T(8,128)(2,1)S(1)}, bf16[32,16,768]{2,1,0:T(8,128)(2,1)S(1)}, u32[]{:S(2)}, u32[]{:S(2)}) %collective-permute-start.2) | collective-permute-done | bytes 786464 | tf_op jit(solution)/shard_map/ppermute | solution.py:138
  71.6 1.1 %bitcast_add_fusion = bf16[32,16,768]{2,1,0:T(8,128)(2,1)} fusion(bf16[32,16,768]{2,1,0:T(8,128)(2,1)S(1)} %collective-permute-done.2, bf16[4,2,4,16,768]{4,3,2,1,0:T(8,128)(2,1)S(1)} %shard_map.50), kind=kLoop, calls=%fused_computation | loop fusion | flops 393216 | bytes 2359296 | tf_op jit(solution)/shard_map/add | solution.py:183
  72.6 8.1 %all-to-all-start.1 = ((bf16[32,16,768]{2,1,0:T(8,128)(2,1)}), bf16[32,16,768]{2,1,0:T(8,128)(2,1)S(1)}, u32[]{:S(2)}, u32[]{:S(2)}) async-start(bf16[32,16,768]{2,1,0:T(8,128)(2,1)} %bitcast_add_fusion), calls=%async_computation.1 | async-start | bytes 1572864 | tf_op jit(solution)/shard_map/all_to_all | solution.py:34
  80.7 0.0 collective-permute-done.3
  80.7 2.0 %shard_map.54 = bf16[384,768]{1,0:T(8,128)(2,1)S(1)} custom-call(s32[3]{0:T(128)S(1)} %pad_add_fusion.refs_0_.s_ref, bf16[4,2,4,16,768]{4,3,2,1,0:T(8,128)(2,1)S(1)} %bitcast.55, bf16[4,2,4,16,768]{4,3,2,1,0:T(8,128)(2,1)} %bitcast.20.refs_2_, bf16[4,4,2,16,768]{4,3,2,1,0:T(8,128)(2,1)S(1)} %bitcast.49, bf16[4,4,2,16,768]{4,3,2,1,0:T(8,128)(2,1)S(1)} %bitcast.53), custom_call_target="tpu_custom_call" | custom-call | flops 10000000000 | tf_op jit(solution)/shard_map/pallas_call | solution.py:41
  82.7 1.9 %collective-permute-start.4 = (bf16[384,768]{1,0:T(8,128)(2,1)S(1)}, bf16[384,768]{1,0:T(8,128)(2,1)S(1)}, u32[]{:S(2)}, u32[]{:S(2)}) collective-permute-start(bf16[384,768]{1,0:T(8,128)(2,1)S(1)} %shard_map.54), channel_id=1, source_target_pairs={{0,256},{32,288},{64,320},{96,352},{128,384},{160,416},{192,448},{... | collective-permute-start | bytes 1769480 | tf_op jit(solution)/shard_map/ppermute | solution.py:129
  84.7 2.0 %shard_map.53.a_ref = f32[384,768]{1,0:T(8,128)S(1)} custom-call(s32[3]{0:T(128)S(1)} %pad_add_fusion.refs_0_.s_ref, bf16[4,2,4,16,768]{4,3,2,1,0:T(8,128)(2,1)S(1)} %bitcast.56, bf16[4,2,4,16,768]{4,3,2,1,0:T(8,128)(2,1)} %bitcast.20.refs_2_, bf16[4,4,2,16,768]{4,3,2,1,0:T(8,128)(2,1)S(1)} %bitcast.50, bf16[4,4,2,16,768]{4,3,2,1,0:T(8,128)(2,1)S(1)} %bitcast.54), custom_call_target="tpu_custom_call" | custom-call | tf_op jit(solution)/shard_map/pallas_call | solution.py:41
  86.6 12.7 %collective-permute-done.4.b_ref = bf16[384,768]{1,0:T(8,128)(2,1)S(1)} collective-permute-done((bf16[384,768]{1,0:T(8,128)(2,1)S(1)}, bf16[384,768]{1,0:T(8,128)(2,1)S(1)}, u32[]{:S(2)}, u32[]{:S(2)}) %collective-permute-start.4) | collective-permute-done | bytes 589856 | tf_op jit(solution)/shard_map/ppermute | solution.py:129
  99.3 1.5 %shard_map.55 = bf16[384,768]{1,0:T(8,128)(2,1)} custom-call(s32[3]{0:T(128)S(1)} %pad_add_fusion.refs_0_.s_ref, f32[384,768]{1,0:T(8,128)S(1)} %shard_map.53.a_ref, bf16[384,768]{1,0:T(8,128)(2,1)S(1)} %collective-permute-done.4.b_ref), custom_call_target="tpu_custom_call" | custom-call | tf_op jit(solution)/shard_map/pallas_call | solution.py:41
  100.8 2.9 %all-to-all-done.1 = bf16[32,16,768]{2,1,0:T(8,128)(2,1)S(1)} async-done(((bf16[32,16,768]{2,1,0:T(8,128)(2,1)}), bf16[32,16,768]{2,1,0:T(8,128)(2,1)S(1)}, u32[]{:S(2)}, u32[]{:S(2)}) %all-to-all-start.1) | async-done | bytes 786464 | tf_op jit(solution)/shard_map/all_to_all | solution.py:34
  103.6 1.3 %shard_map.52 = bf16[16,6144]{1,0:T(8,128)(2,1)} custom-call(s32[3]{0:T(128)S(1)} %pad_add_fusion.refs_0_.s_ref, bf16[4,2,4,16,768]{4,3,2,1,0:T(8,128)(2,1)S(1)} %bitcast.57), custom_call_target="tpu_custom_call" | custom-call | tf_op jit(solution)/shard_map/pallas_call | solution.py:41
  (8 shorter events, 0.0 us)
Async XLA Ops:
  1.6 12.2 %copy-start.1 = (bf16[32,768]{1,0:T(8,128)(2,1)S(1)}, bf16[32,768]{1,0:T(8,128)(2,1)}, u32[]{:S(2)}) copy-start(bf16[32,768]{1,0:T(8,128)(2,1)} %param.4) | copy-start | bytes 147460
  1.7 29.8 %copy-start = (bf16[1,384,768]{2,1,0:T(8,128)(2,1)S(1)}, bf16[1,384,768]{2,1,0:T(8,128)(2,1)}, u32[]{:S(2)}) copy-start(bf16[1,384,768]{2,1,0:T(8,128)(2,1)} %param.5) | copy-start | bytes 1769476
  2.6 43.9 %all-to-all-start = ((bf16[32,16,768]{2,1,0:T(8,128)(2,1)}), bf16[32,16,768]{2,1,0:T(8,128)(2,1)S(1)}, u32[]{:S(2)}, u32[]{:S(2)}) async-start(bf16[32,16,768]{2,1,0:T(8,128)(2,1)} %bitcast.12), calls=%async_computation | async-start | bytes 1572864 | tf_op jit(solution)/shard_map/all_to_all | solution.py:34
  31.5 15.0 %collective-permute-start = (bf16[384,768]{1,0:T(8,128)(2,1)S(1)}, bf16[384,768]{1,0:T(8,128)(2,1)S(1)}, u32[]{:S(2)}, u32[]{:S(2)}) collective-permute-start(bf16[384,768]{1,0:T(8,128)(2,1)S(1)} %bitcast.58), channel_id=1, source_target_pairs={{0,256},{32,288},{64,320},{96,352},{128,384},{160,416},{192,448},{... | collective-permute-start | bytes 1769480 | tf_op jit(solution)/shard_map/ppermute | solution.py:129
  46.5 9.6 %collective-permute-start.1 = (bf16[512,768]{1,0:T(8,128)(2,1)S(1)}, bf16[512,768]{1,0:T(8,128)(2,1)S(1)}, u32[]{:S(2)}, u32[]{:S(2)}) collective-permute-start(bf16[512,768]{1,0:T(8,128)(2,1)S(1)} %all_gather.7), channel_id=1, source_target_pairs={{0,32},{32,0},{64,96},{96,64},{128,160},{160,128},{192,224},{224,1... | collective-permute-start | bytes 2359304 | tf_op jit(solution)/shard_map/ppermute | solution.py:125
  57.6 13.9 %collective-permute-start.2 = (bf16[32,16,768]{2,1,0:T(8,128)(2,1)S(1)}, bf16[32,16,768]{2,1,0:T(8,128)(2,1)S(1)}, u32[]{:S(2)}, u32[]{:S(2)}) collective-permute-start(bf16[32,16,768]{2,1,0:T(8,128)(2,1)S(1)} %bitcast.61), channel_id=1, source_target_pairs={{0,4},{4,0},{8,12},{12,8},{16,20},{20,16},{24,28},{28,24},{32,60},... | collective-permute-start | bytes 2359304 | tf_op jit(solution)/shard_map/ppermute | solution.py:138
  62.0 18.7 %collective-permute-start.3 = (bf16[32,16,768]{2,1,0:T(8,128)(2,1)S(1)}, bf16[32,16,768]{2,1,0:T(8,128)(2,1)}, u32[]{:S(2)}, u32[]{:S(2)}) collective-permute-start(bf16[32,16,768]{2,1,0:T(8,128)(2,1)S(1)} %all-to-all-done), channel_id=1, source_target_pairs={{0,4},{4,0},{8,12},{12,8},{16,20},{20,16},{24,28},{28,24},{32,60},... | collective-permute-start | bytes 2359304 | tf_op jit(solution)/shard_map/ppermute | solution.py:138
  72.6 31.0 %all-to-all-start.1 = ((bf16[32,16,768]{2,1,0:T(8,128)(2,1)}), bf16[32,16,768]{2,1,0:T(8,128)(2,1)S(1)}, u32[]{:S(2)}, u32[]{:S(2)}) async-start(bf16[32,16,768]{2,1,0:T(8,128)(2,1)} %bitcast_add_fusion), calls=%async_computation.1 | async-start | bytes 1572864 | tf_op jit(solution)/shard_map/all_to_all | solution.py:34
  82.7 16.6 %collective-permute-start.4 = (bf16[384,768]{1,0:T(8,128)(2,1)S(1)}, bf16[384,768]{1,0:T(8,128)(2,1)S(1)}, u32[]{:S(2)}, u32[]{:S(2)}) collective-permute-start(bf16[384,768]{1,0:T(8,128)(2,1)S(1)} %shard_map.54), channel_id=1, source_target_pairs={{0,256},{32,288},{64,320},{96,352},{128,384},{160,416},{192,448},{... | collective-permute-start | bytes 1769480 | tf_op jit(solution)/shard_map/ppermute | solution.py:129
